TPU v7x, 32 devices: a whole 2x2x4 slice. The times are simulated.
32 devices in a mesh: rep: 4 (over y, x), exp: 8 (over z, core).
Axes of the slice: x: 2, y: 2, z: 4, core: 2. Of those that a mesh axis runs over, the one named last changes fastest.
Arguments:
- tokens: bfloat16 [1024, 3584], P(('rep', 'exp')), parts along dimension 0, may hold values from -6 to 6
- expert_ids: int32 [1024, 8], P(('rep', 'exp')), parts along dimension 0, may hold values from 0 to 383, all different within a row; in each aligned block of 32 rows (0 to 31, 32 to 63, ...) at most 2 rows name the same one
- gate_scores: float32 [1024, 8], P(('rep', 'exp')), parts along dimension 0, may hold values from 0.02 to 0.4
- gate_weight: bfloat16 [3584, 16384], P(None, 'exp'), may hold values from -0.09375 to 0.09375
- up_weight: bfloat16 [3584, 16384], P(None, 'exp'), may hold values from -0.09375 to 0.09375
- down_weight: bfloat16 [16384, 3584], P('exp'), may hold values from -0.125 to 0.125
Outputs:
- combined: bfloat16 [1024, 3584], P(('rep', 'exp')), parts along dimension 0
- expert_load: float32 [1536], P('rep'), parts along dimension 0
There are 4 independent parts, one for each index of `rep`. A program takes and returns all parts, laid end to end along the dimension named above; an argument that names none is the same for every part. Nothing has to cross between parts.
Inputs may be any that keep to these rules, and one draw needn't show every extreme that they name: `expert_ids`: each row names 8 different experts. Among the rows of one device no expert is named by more than 2 rows, a bound that some block reaches.
All inputs are finite; a program needn't handle non-finite values.
Results may differ from a plain program's by a relative error of at most 0.0057.
Values may be sent and summed in bfloat16 or wider, within the bound.
A program may use at most 128 MiB of HBM per device.

v0:
```python
import jax
import jax.numpy as jnp
from jax import lax
from jax.sharding import PartitionSpec as P

FF = 2048
EXPERTS_ALL = 384
EXPERTS = 8
CAP = 2


def expert_rows(arrived, gate_weight, up_weight, down_weight):
    flat_rows = arrived.reshape(-1, arrived.shape[-1])
    gate_act = jnp.dot(flat_rows, gate_weight, preferred_element_type=jnp.float32)
    up_act = jnp.dot(flat_rows, up_weight, preferred_element_type=jnp.float32)
    hidden = (jax.nn.silu(gate_act) * up_act).astype(jnp.bfloat16)
    partial_value = jnp.dot(hidden, down_weight, preferred_element_type=jnp.float32).astype(
        jnp.bfloat16
    )
    return partial_value.reshape(arrived.shape)


def shards(tokens, expert_ids, gate_scores, gate_weight, up_weight, down_weight):
    dev_count = lax.axis_size("exp")
    hid_dev = gate_weight.shape[1]
    spread = FF // hid_dev
    tok_rows = tokens.shape[0]
    feat_width = tokens.shape[1]
    matches = expert_ids[:, :, None] == jnp.arange(EXPERTS_ALL, dtype=jnp.int32)[None, None, :]
    onehot = jnp.where(matches, 1.0, 0.0).astype(jnp.float32)
    routed_mass = jnp.einsum("tk,tke->e", gate_scores, onehot, precision=lax.Precision.HIGHEST)
    expert_load = lax.psum(routed_mass, "exp")
    window_match = matches[:, :, :EXPERTS]
    win_hits = jnp.any(window_match, axis=1)
    win_gate = jnp.sum(jnp.where(window_match, gate_scores[:, :, None], 0.0), axis=1)
    position = jnp.cumsum(win_hits.astype(jnp.int32), axis=0) - 1
    slot_ids = jnp.arange(CAP, dtype=jnp.int32)
    placed = win_hits[:, :, None] & (position[:, :, None] == slot_ids[None, None, :])
    placing = placed.reshape(tok_rows, EXPERTS * CAP)
    picker = jnp.where(placing.T, 1.0, 0.0).astype(jnp.bfloat16)
    outgoing = jnp.dot(picker, tokens, preferred_element_type=jnp.float32).astype(jnp.bfloat16)
    outgoing = jnp.broadcast_to(
        outgoing.reshape(EXPERTS, 1, CAP, feat_width), (EXPERTS, spread, CAP, feat_width)
    )
    outgoing = outgoing.reshape(dev_count, CAP, feat_width)
    arrived = lax.all_to_all(outgoing, "exp", split_axis=0, concat_axis=0, tiled=True)
    returned = lax.all_to_all(
        expert_rows(arrived, gate_weight, up_weight, down_weight),
        "exp",
        split_axis=0,
        concat_axis=0,
        tiled=True,
    )
    summed = jnp.sum(returned.reshape(EXPERTS, spread, CAP, feat_width), axis=1, dtype=jnp.float32)
    summed = summed.reshape(EXPERTS * CAP, feat_width)
    weights_slot = jnp.where(placed, win_gate[:, :, None], 0.0).reshape(tok_rows, EXPERTS * CAP)
    combined = jnp.dot(weights_slot, summed, precision=lax.Precision.HIGHEST).astype(jnp.bfloat16)
    return (combined, expert_load)


def solution(mesh):
    return jax.shard_map(
        shards,
        mesh=mesh,
        in_specs=(
            P(("rep", "exp"), None),
            P(("rep", "exp"), None),
            P(("rep", "exp"), None),
            P(None, "exp"),
            P(None, "exp"),
            P("exp", None),
        ),
        out_specs=(P(("rep", "exp"), None), P("rep")),
        check_vma=False,
    )
```

profile of v0, /device:TPU:0, one launch (start us, length us, event | category | flops | bytes accessed | tf_op | source)
XLA Modules:
  0.0 60.1 jit_solution(4591416866055403861)
XLA Ops:
  0.6 0.0 copy-start
  0.7 0.1 eq.45
  0.7 0.9 %iota_compare_fusion = pred[32,8,384]{0,2,1:T(8,128)(4,1)S(1)} fusion(s32[32,8]{0,1:T(8,128)} %param.7), kind=kLoop, calls=%fused_computation.8 | loop fusion | flops 98304 | bytes 99328 | tf_op jit(solution)/shard_map/eq | solution.py:29
  1.7 0.1 copy.25
  1.8 0.1 reduce_window_sum.11
  1.9 0.1 copy.26
  2.0 0.0 copy-done
  2.0 0.2 convolution_convert_fusion.1
  2.2 0.7 %reshape_reshape.3 = bf16[8,2,3584]{2,1,0:T(2,128)(2,1)} reshape(bf16[16,3584]{1,0:T(8,128)(2,1)S(1)} %convolution_convert_fusion.1) | data formatting | bytes 229376 | tf_op jit(solution)/shard_map/reshape;reshape | solution.py:45
  2.9 6.3 %all-to-all-start = ((bf16[8,2,3584]{2,1,0:T(2,128)(2,1)}), bf16[8,2,3584]{2,1,0:T(2,128)(2,1)S(1)}, u32[]{:S(2)}, u32[]{:S(2)}) async-start(bf16[8,2,3584]{2,1,0:T(2,128)(2,1)} %reshape_reshape.3), calls=%async_computation | async-start | bytes 229376 | tf_op jit(solution)/shard_map/all_to_all | solution.py:46
  9.2 2.2 %fusion.4 = f32[384]{0:T(512)S(1)} fusion(f32[32,8,1]{0,2,1:T(1,128)} %bitcast.18, s32[32,8]{0,1:T(8,128)} %param.7), kind=kOutput, calls=%fused_computation.9 | convolution fusion | flops 1376256 | bytes 3584 | tf_op jit(solution)/shard_map/tk,tke->e/dot_general | solution.py:31
  11.4 17.7 %psum.7 = f32[384]{0:T(512)} all-reduce(f32[384]{0:T(512)S(1)} %fusion.4), channel_id=1, replica_groups=mesh['rep'=4,'exp'=8] {'exp'}, use_global_device_ids=true, to_apply=%region_3.4 | all-reduce | flops 384 | bytes 3072 | tf_op jit(solution)/shard_map/psum | solution.py:32
  29.2 0.7 %select_reduce_fusion = f32[32,8]{0,1:T(8,128)S(1)} fusion(pred[32,8,384]{0,2,1:T(8,128)(4,1)S(1)} %iota_compare_fusion, f32[32,8]{0,1:T(8,128)} %param.8), kind=kLoop, calls=%fused_computation.19 | loop fusion | flops 3840 | bytes 4096 | tf_op jit(solution)/shard_map/reduce_sum | solution.py:35
  29.9 0.0 all-to-all-done
  29.9 7.2 %fusion.25 = f32[16,2048]{1,0:T(8,128)S(1)} fusion(bf16[16,3584]{1,0:T(8,128)(2,1)S(1)} %reshape.33, bf16[3584,2048]{1,0:T(8,128)(2,1)} %param.9), kind=kOutput, calls=%fused_computation.33 | convolution fusion | flops 234881024 | bytes 14925824 | tf_op jit(solution)/shard_map/dot_general | solution.py:14
  37.1 11.4 %convolution_convert_fusion = bf16[16,3584]{1,0:T(8,128)(2,1)S(1)} fusion(bf16[2048,3584]{1,0:T(8,128)(2,1)} %param.11, bf16[16,3584]{1,0:T(8,128)(2,1)S(1)} %reshape.33, bf16[3584,2048]{1,0:T(8,128)(2,1)} %param.10, f32[16,2048]{1,0:T(8,128)S(1)} %fusion.25), kind=kOutput, calls=%fused_computation.2 | convolution fusion | flops 470016000 | bytes 29720576 | tf_op jit(solution)/shard_map/dot_general | solution.py:17
  48.5 0.7 %reshape.34 = bf16[8,2,3584]{2,1,0:T(2,128)(2,1)} reshape(bf16[16,3584]{1,0:T(8,128)(2,1)S(1)} %convolution_convert_fusion) | data formatting | bytes 229376 | tf_op jit(solution)/shard_map/reshape | solution.py:20
  49.2 3.4 %all-to-all-start.1 = ((bf16[8,2,3584]{2,1,0:T(2,128)(2,1)}), bf16[8,2,3584]{2,1,0:T(2,128)(2,1)S(1)}, u32[]{:S(2)}, u32[]{:S(2)}) async-start(bf16[8,2,3584]{2,1,0:T(2,128)(2,1)} %reshape.34), calls=%async_computation.1 | async-start | bytes 229376 | tf_op jit(solution)/shard_map/all_to_all | solution.py:47
  52.6 6.5 %all-to-all-done.1 = bf16[8,2,3584]{2,1,0:T(2,128)(2,1)S(1)} async-done(((bf16[8,2,3584]{2,1,0:T(2,128)(2,1)}), bf16[8,2,3584]{2,1,0:T(2,128)(2,1)S(1)}, u32[]{:S(2)}, u32[]{:S(2)}) %all-to-all-start.1) | async-done | bytes 114720 | tf_op jit(solution)/shard_map/all_to_all | solution.py:47
  59.1 1.1 %fusion = bf16[32,3584]{1,0:T(8,128)(2,1)} fusion(bf16[8,2,3584]{2,1,0:T(2,128)(2,1)S(1)} %all-to-all-done.1, f32[32,8,2]{0,2,1:T(2,128)S(1)} %and_select_fusion), kind=kOutput, calls=%fused_computation.1 | convolution fusion | flops 22134784 | bytes 346112 | tf_op jit(solution)/shard_map/dot_general | solution.py:57
  (9 shorter events, 0.1 us)
Async XLA Ops:
  0.6 1.3 %copy-start = (bf16[32,3584]{1,0:T(8,128)(2,1)S(1)}, bf16[32,3584]{1,0:T(8,128)(2,1)}, u32[]{:S(2)}) copy-start(bf16[32,3584]{1,0:T(8,128)(2,1)} %param.6) | copy-start | bytes 688132
  2.9 27.0 %all-to-all-start = ((bf16[8,2,3584]{2,1,0:T(2,128)(2,1)}), bf16[8,2,3584]{2,1,0:T(2,128)(2,1)S(1)}, u32[]{:S(2)}, u32[]{:S(2)}) async-start(bf16[8,2,3584]{2,1,0:T(2,128)(2,1)} %reshape_reshape.3), calls=%async_computation | async-start | bytes 229376 | tf_op jit(solution)/shard_map/all_to_all | solution.py:46
  49.2 9.9 %all-to-all-start.1 = ((bf16[8,2,3584]{2,1,0:T(2,128)(2,1)}), bf16[8,2,3584]{2,1,0:T(2,128)(2,1)S(1)}, u32[]{:S(2)}, u32[]{:S(2)}) async-start(bf16[8,2,3584]{2,1,0:T(2,128)(2,1)} %reshape.34), calls=%async_computation.1 | async-start | bytes 229376 | tf_op jit(solution)/shard_map/all_to_all | solution.py:47
where the time goes:
time: 60.7 us; the launch traced here: 60.1 us
  matrix products  22.1 us (36%)
  blocking collectives  17.7 us (29%)
  starting transfers between devices  9.69 us (16%)
  waiting for transfers between devices  6.47 us (11%)
  other arithmetic  1.73 us (3%)
  local copies, waits for them, and re-layouts  1.7 us (3%)
  between operations  0.73 us (1%)
    psum x1, blocking collectives, shards(): expert_load = lax.psum(routed_mass, 'exp')  17.7 us
    dot_general x1, matrix products, expert_rows(): jnp.dot(hidden, down_weight, preferred_element_type=jnp.float32)  11.4 us
    dot_general x1, matrix products, expert_rows(): jnp.dot(flat_rows, gate_weight, preferred_element_type=jnp.float32)  7.18 us
    all_to_all x1, waiting for transfers between devices, shards(): lax.all_to_all(expert_rows(arrived, gate_weight, up_weight, down_weight),...  6.47 us
    all_to_all x1, starting transfers between devices, shards(): lax.all_to_all(outgoing, 'exp', split_axis=0, concat_axis=0, tiled=True)  6.33 us
    all_to_all x1, starting transfers between devices, shards(): lax.all_to_all(expert_rows(arrived, gate_weight, up_weight, down_weight),...  3.37 us
    dot_general x1, matrix products, shards(): jnp.einsum('tk,tke->e', gate_scores, onehot, precision=lax.Precision.HIGH...  2.22 us
  transfers between devices with their start and end apart: 2, of which 1 were waited for; matrix products, arithmetic and copies ran while one was open for 5% of the time, Pallas kernels for 0%

commit v1 on v0

v1 whole, which is shorter than its diff:
```python
import functools

import jax
import jax.numpy as jnp
from jax import lax
from jax.experimental import pallas as pl
from jax.experimental.pallas import tpu as pltpu
from jax.sharding import PartitionSpec as P

FF = 2048
EXPERTS_ALL = 384
CAP = 2
SLAB = 16
GROUP = 8
MESH = pl.DeviceIdType.MESH
BF16 = jnp.bfloat16
F32 = jnp.float32


def dot(a, b):
    return jnp.dot(a, b, preferred_element_type=F32)


def iota(shape, dim):
    return lax.broadcasted_iota(jnp.int32, shape, dim)


def one_hot(mask):
    return jnp.where(mask, 1.0, 0.0).astype(BF16)


def slab_place(i, segs):
    dev, seg, row = i // SLAB, (i % SLAB) // CAP, i % CAP
    return jnp.where(seg < segs, seg * (GROUP * CAP) + dev * CAP + row, -1)


def kernel(
    cfg,
    tokens_hbm, ids_hbm, scores_hbm, gate_hbm, up_hbm, down_hbm,
    out_ref, load_ref,
    tokens_v, ids_v, scores_v, gate_v, up_v, down_v,
    send_v, arrived_v, x_v, back_v, returned_v, mass_v, mixing_v, hidden_v,
    small_sem, gate_sem, up_sem, down_sem,
    send_sem, recv_sem, mass_send_sem, mass_recv_sem, back_send_sem, back_recv_sem,
):
    n, spread, segs, seg_w, pieces, piece_w, k_parts, k_rows = cfg
    groups = n // GROUP
    tok_rows, top = ids_v.shape
    lanes = mixing_lanes(n)
    me = lax.axis_index("exp")
    back_w = piece_w // segs

    small = [
        pltpu.make_async_copy(ids_hbm, ids_v, small_sem.at[0]),
        pltpu.make_async_copy(scores_hbm, scores_v, small_sem.at[1]),
        pltpu.make_async_copy(tokens_hbm, tokens_v, small_sem.at[2]),
    ]
    for copy in small:
        copy.start()

    def gate_copy(s):
        return pltpu.make_async_copy(
            gate_hbm.at[pl.ds(s * seg_w, seg_w), :], gate_v.at[s], gate_sem.at[s]
        )

    def up_copy(s):
        return pltpu.make_async_copy(
            up_hbm.at[pl.ds(s * seg_w, seg_w), :], up_v.at[s], up_sem.at[s]
        )

    def down_copy(p, k):
        return pltpu.make_async_copy(
            down_hbm.at[pl.ds(k * k_rows, k_rows), pl.ds(p * piece_w, piece_w)],
            down_v.at[p * k_parts + k],
            down_sem.at[p * k_parts + k],
        )

    for s in range(segs):
        gate_copy(s).start()
        up_copy(s).start()
    for p in range(pieces):
        for k in range(k_parts):
            down_copy(p, k).start()

    def others(body):
        def step(i, carry):
            body(lax.rem(me + i, n))
            return carry

        lax.fori_loop(1, n, step, 0, unroll=n <= 16)

    barrier = pltpu.get_barrier_semaphore()
    others(lambda d: pl.semaphore_signal(barrier, inc=1, device_id={"exp": d}, device_id_type=MESH))

    for copy in small[:2]:
        copy.wait()
    ids = ids_v[...]
    scores = scores_v[...]
    all_ids = iota((tok_rows, EXPERTS_ALL), 1)
    slot = iota((tok_rows, lanes), 1)
    slot_expert = jnp.where(slot < n * CAP, slot // (CAP * spread), -1)
    mass = jnp.zeros((tok_rows, EXPERTS_ALL), F32)
    gates = jnp.zeros((tok_rows, lanes), F32)
    hits = jnp.zeros((tok_rows, lanes), F32)
    for k in range(top):
        id_k, score_k = ids[:, k : k + 1], scores[:, k : k + 1]
        mass = mass + jnp.where(id_k == all_ids, score_k, 0.0)
        found = id_k == slot_expert
        gates = gates + jnp.where(found, score_k, 0.0)
        hits = hits + jnp.where(found, 1.0, 0.0)
    earlier = one_hot(iota((tok_rows, tok_rows), 1) < iota((tok_rows, tok_rows), 0))
    position = dot(earlier, hits.astype(BF16))
    placed = (hits > 0.5) & (position == (slot % CAP).astype(F32))
    picker = jnp.transpose(jnp.where(placed, 1.0, 0.0)).astype(BF16)
    mass_v[me] = jnp.sum(mass, axis=0, keepdims=True)

    slab_rows, packed_rows = GROUP * SLAB, segs * GROUP * CAP
    to_slab = one_hot(
        slab_place(iota((slab_rows, packed_rows), 0), segs) == iota((slab_rows, packed_rows), 1)
    )
    from_slab = one_hot(
        slab_place(iota((packed_rows, slab_rows), 1), segs) == iota((packed_rows, slab_rows), 0)
    )
    small[2].wait()
    tokens = tokens_v[...]
    for g in range(groups):
        rows = picker[g * GROUP * CAP : (g + 1) * GROUP * CAP]
        picked = dot(rows, tokens).astype(BF16)
        packed = jnp.concatenate([picked[:, s * seg_w : (s + 1) * seg_w] for s in range(segs)], axis=0)
        slabs = dot(to_slab, packed).astype(BF16)
        send_v[g * GROUP : (g + 1) * GROUP] = slabs.reshape(GROUP, SLAB, seg_w)

    def token_copy(d, src):
        return pltpu.make_async_remote_copy(
            src_ref=send_v.at[d], dst_ref=arrived_v.at[src],
            send_sem=send_sem.at[d], recv_sem=recv_sem.at[src],
            device_id={"exp": d}, device_id_type=MESH,
        )

    def mass_copy(d, src):
        return pltpu.make_async_remote_copy(
            src_ref=mass_v.at[me], dst_ref=mass_v.at[src],
            send_sem=mass_send_sem.at[d], recv_sem=mass_recv_sem.at[src],
            device_id={"exp": d}, device_id_type=MESH,
        )

    pl.semaphore_wait(barrier, n - 1)
    others(lambda d: token_copy(d, me).start())
    others(lambda d: mass_copy(d, me).start())
    arrived_v[me] = send_v[me]

    weights = jnp.where(placed, gates, 0.0)
    weights_hi = weights.astype(BF16)
    weights_lo = (weights - weights_hi.astype(F32)).astype(BF16)
    slab_lane = iota((lanes, slab_rows), 1)
    lane_seg = (iota((tok_rows, slab_rows), 1) % SLAB) // CAP
    for g in range(groups):
        slot_of = g * GROUP * CAP + slab_lane // SLAB * CAP + slab_lane % CAP
        spreading = one_hot(iota((lanes, slab_rows), 0) == slot_of)
        for part, term in enumerate((weights_hi, weights_lo)):
            wide = dot(term, spreading)
            for s in range(segs):
                mixing_v[
                    g, s * tok_rows : (s + 1) * tok_rows, part * slab_rows : (part + 1) * slab_rows
                ] = jnp.where(lane_seg == s, wide, 0.0).astype(BF16)

    others(lambda d: token_copy(d, d).wait_recv())
    for g in range(groups):
        slabs = arrived_v[g * GROUP : (g + 1) * GROUP].reshape(slab_rows, seg_w)
        packed = dot(from_slab, slabs).astype(BF16)
        for s in range(segs):
            x_v[s, g * GROUP * CAP : (g + 1) * GROUP * CAP] = packed[
                s * GROUP * CAP : (s + 1) * GROUP * CAP
            ]

    def gate_up(s, sums):
        gate_sum, up_sum = sums
        rows = x_v[s]
        gate_copy(s).wait()
        gate_sum = gate_sum + dot(rows, gate_v[s])
        up_copy(s).wait()
        up_sum = up_sum + dot(rows, up_v[s])
        return gate_sum, up_sum

    zero = jnp.zeros((n * CAP, k_parts * k_rows), F32)
    gate_sum, up_sum = lax.fori_loop(0, segs, gate_up, (zero, zero))
    hidden = (gate_sum / (1.0 + jnp.exp(-gate_sum)) * up_sum).astype(BF16)
    for k in range(k_parts):
        hidden_v[k] = hidden[:, k * k_rows : (k + 1) * k_rows]

    def back_copy(p, d, src):
        return pltpu.make_async_remote_copy(
            src_ref=back_v.at[p, d], dst_ref=returned_v.at[p, src],
            send_sem=back_send_sem.at[p, d], recv_sem=back_recv_sem.at[p, src],
            device_id={"exp": d}, device_id_type=MESH,
        )

    for p in range(pieces):

        def down(k, total, p=p):
            down_copy(p, k).wait()
            return total + dot(hidden_v[k], down_v[p * k_parts + k])

        total = lax.fori_loop(0, k_parts, down, jnp.zeros((n * CAP, piece_w), F32))
        partial_value = total.astype(BF16)
        for g in range(groups):
            rows = partial_value[g * GROUP * CAP : (g + 1) * GROUP * CAP]
            packed = jnp.concatenate(
                [rows[:, s * back_w : (s + 1) * back_w] for s in range(segs)], axis=0
            )
            slabs = dot(to_slab, packed).astype(BF16)
            back_v[p, g * GROUP : (g + 1) * GROUP] = slabs.reshape(GROUP, SLAB, back_w)
        others(lambda d, p=p: back_copy(p, d, me).start())
        returned_v[p, me] = back_v[p, me]

    others(lambda d: mass_copy(d, d).wait_recv())
    load_ref[...] = jnp.sum(mass_v[...], axis=0)

    for p in range(pieces):
        others(lambda d, p=p: back_copy(p, d, d).wait_recv())
        mixed = jnp.zeros((segs * tok_rows, back_w), F32)
        for g in range(groups):
            slabs = returned_v[p, g * GROUP : (g + 1) * GROUP].reshape(slab_rows, back_w)
            mixed = mixed + dot(mixing_v[g], jnp.concatenate([slabs, slabs], axis=0))
        for s in range(segs):
            low = p * piece_w + s * back_w
            out_ref[:, low : low + back_w] = mixed[s * tok_rows : (s + 1) * tok_rows].astype(BF16)

    others(lambda d: token_copy(d, d).wait_send())
    others(lambda d: mass_copy(d, d).wait_send())
    for p in range(pieces):
        others(lambda d, p=p: back_copy(p, d, d).wait_send())


def mixing_lanes(n):
    return -(-n * CAP // 128) * 128


def shards(tokens, expert_ids, gate_scores, gate_weight, up_weight, down_weight):
    n = lax.axis_size("exp")
    tok_rows, width = tokens.shape
    hid_dev = gate_weight.shape[1]
    spread = FF // hid_dev
    tiles = width // 128
    segs = max(s for s in range(1, SLAB // CAP + 1) if tiles % s == 0)
    seg_w = width // segs
    pieces = 2 if seg_w % 256 == 0 else 1
    piece_w = width // pieces
    k_parts = 4 if hid_dev % 512 == 0 else 1
    k_rows = hid_dev // k_parts
    groups = n // GROUP
    cfg = (n, spread, segs, seg_w, pieces, piece_w, k_parts, k_rows)
    dma = pltpu.SemaphoreType.DMA
    scratch = [
        pltpu.VMEM(tokens.shape, BF16),
        pltpu.VMEM(expert_ids.shape, jnp.int32),
        pltpu.VMEM(gate_scores.shape, F32),
        pltpu.VMEM((segs, seg_w, hid_dev), BF16),
        pltpu.VMEM((segs, seg_w, hid_dev), BF16),
        pltpu.VMEM((pieces * k_parts, k_rows, piece_w), BF16),
        pltpu.VMEM((n, SLAB, seg_w), BF16),
        pltpu.VMEM((n, SLAB, seg_w), BF16),
        pltpu.VMEM((segs, n * CAP, seg_w), BF16),
        pltpu.VMEM((pieces, n, SLAB, piece_w // segs), BF16),
        pltpu.VMEM((pieces, n, SLAB, piece_w // segs), BF16),
        pltpu.VMEM((n, 1, EXPERTS_ALL), F32),
        pltpu.VMEM((groups, segs * tok_rows, 2 * GROUP * SLAB), BF16),
        pltpu.VMEM((k_parts, n * CAP, k_rows), BF16),
        dma((3,)),
        dma((segs,)),
        dma((segs,)),
        dma((pieces * k_parts,)),
        dma((n,)),
        dma((n,)),
        dma((n,)),
        dma((n,)),
        dma((pieces, n)),
        dma((pieces, n)),
    ]
    combined, load = pl.pallas_call(
        functools.partial(kernel, cfg),
        out_shape=(
            jax.ShapeDtypeStruct(tokens.shape, BF16),
            jax.ShapeDtypeStruct((1, EXPERTS_ALL), F32),
        ),
        in_specs=[pl.BlockSpec(memory_space=pl.ANY)] * 6,
        out_specs=(pl.BlockSpec(memory_space=pltpu.VMEM), pl.BlockSpec(memory_space=pltpu.VMEM)),
        scratch_shapes=scratch,
        compiler_params=pltpu.CompilerParams(
            collective_id=0, has_side_effects=True, vmem_limit_bytes=56 * 1024 * 1024
        ),
    )(tokens, expert_ids, gate_scores, gate_weight, up_weight, down_weight)
    return (combined, load.reshape(EXPERTS_ALL))


def solution(mesh):
    return jax.shard_map(
        shards,
        mesh=mesh,
        in_specs=(
            P(("rep", "exp"), None),
            P(("rep", "exp"), None),
            P(("rep", "exp"), None),
            P(None, "exp"),
            P(None, "exp"),
            P("exp", None),
        ),
        out_specs=(P(("rep", "exp"), None), P("rep")),
        check_vma=False,
    )
```

time: 60.7 us -> 39.7 us (0.65)
  Pallas kernels: 0 us -> 33.2 us
  matrix products: 22.1 us -> 0 us
  blocking collectives: 17.7 us -> 0 us
  starting transfers between devices: 9.69 us -> 0 us
  waiting for transfers between devices: 6.47 us -> 0 us
  local copies, waits for them, and re-layouts: 1.7 us -> 4.37 us
    pallas_call x0 -> x1, Pallas kernels: none -> 33.2 us  [shards(): pl.pallas_call(functools.partial(kernel, cfg), out_shape=(jax.ShapeDtypeS...]
    dot_general x5 -> x0, matrix products: 22.1 us -> none  [the longest x1 11.4 us: expert_rows(): jnp.dot(hidden, down_weight, preferred_element_type=jnp.float32)]
    psum x1 -> x0, blocking collectives: 17.7 us -> none  [shards(): expert_load = lax.psum(routed_mass, 'exp')]
    all_to_all x2 -> x0, starting transfers between devices: 9.69 us -> none  [the longest x1 6.33 us: shards(): lax.all_to_all(outgoing, 'exp', split_axis=0, concat_axis=0, tiled=True)]
    all_to_all x2 -> x0, waiting for transfers between devices: 6.47 us -> none  [the longest x1 6.47 us: shards(): lax.all_to_all(expert_rows(arrived, gate_weight, up_weight, down_weight),...]
    unnamed x2 -> x3, local copies, waits for them, and re-layouts: 0.01 us -> 4.37 us
    pallas_call x0 -> x1, other arithmetic: none -> 1.23 us  [shards(): pl.pallas_call(functools.partial(kernel, cfg), out_shape=(jax.ShapeDtypeS...]
    eq x1 -> x0, other arithmetic: 0.93 us -> none  [shards(): expert_ids[:, :, None]]
  transfers between devices with their start and end apart: 2 -> 0, of which waited for: 1 -> 0; matrix products, arithmetic and copies ran while one was open for 5% -> 0% of each run, Pallas kernels for 0% -> 0%
where the time goes in v1:
time: 39.7 us; the launch traced here: 39.4 us
  Pallas kernels  33.2 us (84%)
  local copies, waits for them, and re-layouts  4.37 us (11%)
  other arithmetic  1.23 us (3%)
  between operations  0.64 us (2%)
    pallas_call x1, Pallas kernels, shards(): pl.pallas_call(functools.partial(kernel, cfg), out_shape=(jax.ShapeDtypeS...  33.2 us
    unnamed x3, local copies, waits for them, and re-layouts  4.37 us
    pallas_call x1, other arithmetic, shards(): pl.pallas_call(functools.partial(kernel, cfg), out_shape=(jax.ShapeDtypeS...  1.23 us

profile of v1, /device:TPU:0, one launch (start us, length us, event | category | flops | bytes accessed | tf_op | source)
XLA Modules:
  0.0 39.4 jit_solution(17095928488557962365)
XLA Ops:
  0.6 1.4 %copy.8.ids_hbm = s32[32,8]{1,0:T(8,128)} copy(s32[32,8]{0,1:T(8,128)} %param.7) | data formatting | bytes 2048 | tf_op args[1]
  2.0 1.4 %copy.9.scores_hbm = f32[32,8]{1,0:T(8,128)} copy(f32[32,8]{0,1:T(8,128)} %param.8) | data formatting | bytes 2048 | tf_op args[2]
  3.4 33.2 %shard_map.77 = (bf16[32,3584]{1,0:T(8,128)(2,1)}, f32[1,384]{1,0:T(1,128)}) custom-call(bf16[32,3584]{1,0:T(8,128)(2,1)} %tokens_hbm.1, s32[32,8]{1,0:T(8,128)} %copy.8.ids_hbm, f32[32,8]{1,0:T(8,128)} %copy.9.scores_hbm, bf16[3584,2048]{1,0:T(8,128)(2,1)} %gate_hbm.1, bf16[3584,2048]{1,0:T(8,128)(2,1)} %up_hbm.1, bf16[2048,3584]{1,0:T(8,128)(2,1)} %down_hbm.1), custom_call_target="tpu_custom_call" | custom-call | tf_op jit(solution)/shard_map/pallas_call | solution.py:280
  36.6 1.2 %reduce = f32[384]{0:T(512)} reduce(f32[1,384]{1,0:T(1,128)} %get-tuple-element.5, f32[]{:T(128)} %constant), dimensions={0}, to_apply=%get-tuple-element.5.reduce_sub_computation | reduce | bytes 3076 | tf_op jit(solution)/shard_map/pallas_call | solution.py:280
  37.8 1.6 %copy.11 = bf16[32,3584]{1,0:T(8,128)(2,1)} copy(bf16[32,3584]{1,0:T(8,128)(2,1)} %get-tuple-element.8) | data formatting | bytes 458752

commit v2 on v1

v2 whole, which is shorter than its diff:
```python
import functools

import jax
import jax.numpy as jnp
from jax import lax
from jax.experimental import pallas as pl
from jax.experimental.pallas import tpu as pltpu
from jax.sharding import PartitionSpec as P

FF = 2048
EXPERTS_ALL = 384
CAP = 2
SLAB = 16
GROUP = 8
TILE = 256
MESH = pl.DeviceIdType.MESH
BF16 = jnp.bfloat16
F32 = jnp.float32


def dot(a, b):
    return jnp.dot(a, b, preferred_element_type=F32)


def iota(shape, dim):
    return lax.broadcasted_iota(jnp.int32, shape, dim)


def one_hot(mask):
    return jnp.where(mask, 1.0, 0.0).astype(BF16)


def slab_place(i, segs):
    dev, seg, row = i // SLAB, (i % SLAB) // CAP, i % CAP
    return jnp.where(seg < segs, seg * (GROUP * CAP) + dev * CAP + row, -1)


def kernel(
    cfg,
    tokens_hbm, ids_hbm, scores_hbm, gate_hbm, up_hbm, down_hbm,
    out_ref, load_ref,
    tokens_v, ids_v, scores_v, gate_v, up_v, down_v,
    send_v, arrived_v, back_v, returned_v, mass_v, mixing_v, x_v, gate_sum, up_sum, hidden_v,
    small_sem, gate_sem, up_sem, down_sem,
    send_sem, recv_sem, mass_send_sem, mass_recv_sem, back_send_sem, back_recv_sem,
):
    n, spread, segs, pieces, piece_w, seg_w = cfg
    groups = n // GROUP
    top, tok_rows = ids_v.shape
    lanes = mixing_lanes(n)
    me = lax.axis_index("exp")

    small = [
        pltpu.make_async_copy(ids_hbm, ids_v, small_sem.at[0]),
        pltpu.make_async_copy(scores_hbm, scores_v, small_sem.at[1]),
        pltpu.make_async_copy(tokens_hbm, tokens_v, small_sem.at[2]),
    ]
    for copy in small:
        copy.start()

    def gate_copy(p):
        return pltpu.make_async_copy(
            gate_hbm.at[pl.ds(p * piece_w, piece_w), :], gate_v.at[p], gate_sem.at[p]
        )

    def up_copy(p):
        return pltpu.make_async_copy(
            up_hbm.at[pl.ds(p * piece_w, piece_w), :], up_v.at[p], up_sem.at[p]
        )

    def down_copy(p):
        return pltpu.make_async_copy(
            down_hbm.at[:, pl.ds(p * piece_w, piece_w)], down_v.at[p], down_sem.at[p]
        )

    for p in range(pieces):
        gate_copy(p).start()
        up_copy(p).start()
    for p in range(pieces):
        down_copy(p).start()

    def others(body):
        def step(i, carry):
            body(lax.rem(me + i, n))
            return carry

        lax.fori_loop(1, n, step, 0, unroll=n <= 16)

    barrier = pltpu.get_barrier_semaphore()
    others(lambda d: pl.semaphore_signal(barrier, inc=1, device_id={"exp": d}, device_id_type=MESH))

    for copy in small[:2]:
        copy.wait()
    ids = jnp.transpose(ids_v[...])
    scores = jnp.transpose(scores_v[...])
    all_ids = iota((tok_rows, EXPERTS_ALL), 1)
    slot = iota((tok_rows, lanes), 1)
    slot_expert = jnp.where(slot < n * CAP, slot // (CAP * spread), -1)
    mass = jnp.zeros((tok_rows, EXPERTS_ALL), F32)
    gates = jnp.zeros((tok_rows, lanes), F32)
    hits = jnp.zeros((tok_rows, lanes), F32)
    for k in range(top):
        id_k, score_k = ids[:, k : k + 1], scores[:, k : k + 1]
        mass = mass + jnp.where(id_k == all_ids, score_k, 0.0)
        found = id_k == slot_expert
        gates = gates + jnp.where(found, score_k, 0.0)
        hits = hits + jnp.where(found, 1.0, 0.0)
    earlier = one_hot(iota((tok_rows, tok_rows), 1) < iota((tok_rows, tok_rows), 0))
    position = dot(earlier, hits.astype(BF16))
    placed = (hits > 0.5) & (position == (slot % CAP).astype(F32))
    picker = jnp.transpose(jnp.where(placed, 1.0, 0.0)).astype(BF16)
    mass_v[me] = jnp.sum(mass, axis=0, keepdims=True)

    slab_rows, packed_rows = GROUP * SLAB, segs * GROUP * CAP
    to_slab = one_hot(
        slab_place(iota((slab_rows, packed_rows), 0), segs) == iota((slab_rows, packed_rows), 1)
    )
    from_slab = one_hot(
        slab_place(iota((packed_rows, slab_rows), 1), segs) == iota((packed_rows, slab_rows), 0)
    )

    def pack(rows):
        packed = jnp.concatenate([rows[:, s * seg_w : (s + 1) * seg_w] for s in range(segs)], axis=0)
        return dot(to_slab, packed).astype(BF16).reshape(GROUP, SLAB, seg_w)

    small[2].wait()
    tokens = tokens_v[...]
    for g in range(groups):
        rows = picker[g * GROUP * CAP : (g + 1) * GROUP * CAP]
        picked = dot(rows, tokens).astype(BF16)
        for p in range(pieces):
            slabs = pack(picked[:, p * piece_w : (p + 1) * piece_w])
            send_v[p, g * GROUP : (g + 1) * GROUP] = slabs

    def token_copy(p, d, src):
        return pltpu.make_async_remote_copy(
            src_ref=send_v.at[p, d], dst_ref=arrived_v.at[p, src],
            send_sem=send_sem.at[p, d], recv_sem=recv_sem.at[p, src],
            device_id={"exp": d}, device_id_type=MESH,
        )

    def mass_copy(d, src):
        return pltpu.make_async_remote_copy(
            src_ref=mass_v.at[me], dst_ref=mass_v.at[src],
            send_sem=mass_send_sem.at[d], recv_sem=mass_recv_sem.at[src],
            device_id={"exp": d}, device_id_type=MESH,
        )

    pl.semaphore_wait(barrier, n - 1)
    for p in range(pieces):
        others(lambda d, p=p: token_copy(p, d, me).start())
        arrived_v[p, me] = send_v[p, me]
    others(lambda d: mass_copy(d, me).start())

    weights = jnp.where(placed, gates, 0.0)
    weights_hi = weights.astype(BF16)
    weights_lo = (weights - weights_hi.astype(F32)).astype(BF16)
    slab_lane = iota((lanes, slab_rows), 1)
    lane_seg = (iota((tok_rows, slab_rows), 1) % SLAB) // CAP
    for g in range(groups):
        slot_of = g * GROUP * CAP + slab_lane // SLAB * CAP + slab_lane % CAP
        spreading = one_hot(iota((lanes, slab_rows), 0) == slot_of)
        for part, term in enumerate((weights_hi, weights_lo)):
            wide = dot(term, spreading)
            for s in range(segs):
                mixing_v[
                    g, s * tok_rows : (s + 1) * tok_rows, part * slab_rows : (part + 1) * slab_rows
                ] = jnp.where(lane_seg == s, wide, 0.0).astype(BF16)

    hid_dev = hidden_v.shape[1]
    hid_tile = min(TILE, hid_dev)
    for p in range(pieces):
        others(lambda d, p=p: token_copy(p, d, d).wait_recv())
        for g in range(groups):
            slabs = arrived_v[p, g * GROUP : (g + 1) * GROUP].reshape(slab_rows, seg_w)
            packed = dot(from_slab, slabs).astype(BF16)
            size = GROUP * CAP
            for s in range(segs):
                x_v[g * size : (g + 1) * size, s * seg_w : (s + 1) * seg_w] = packed[
                    s * size : (s + 1) * size
                ]
        gate_copy(p).wait()
        up_copy(p).wait()

        def gate_up(j, carry, p=p):
            cols = pl.ds(pl.multiple_of(j * hid_tile, hid_tile), hid_tile)
            gate_act = dot(x_v[...], gate_v[p, :, cols])
            up_act = dot(x_v[...], up_v[p, :, cols])
            if p > 0:
                gate_act = gate_act + gate_sum[:, cols]
                up_act = up_act + up_sum[:, cols]
            if p < pieces - 1:
                gate_sum[:, cols] = gate_act
                up_sum[:, cols] = up_act
            else:
                silu = gate_act / (1.0 + jnp.exp(-gate_act))
                hidden_v[:, cols] = (silu * up_act).astype(BF16)
            return carry

        lax.fori_loop(0, hid_dev // hid_tile, gate_up, 0)

    def back_copy(p, d, src):
        return pltpu.make_async_remote_copy(
            src_ref=back_v.at[p, d], dst_ref=returned_v.at[p, src],
            send_sem=back_send_sem.at[p, d], recv_sem=back_recv_sem.at[p, src],
            device_id={"exp": d}, device_id_type=MESH,
        )

    for p in range(pieces):
        down_copy(p).wait()
        for s in range(segs):
            cols = slice(s * seg_w, (s + 1) * seg_w)
            x_v[:, cols] = dot(hidden_v[...], down_v[p, :, cols]).astype(BF16)
        for g in range(groups):
            rows = x_v[g * GROUP * CAP : (g + 1) * GROUP * CAP]
            back_v[p, g * GROUP : (g + 1) * GROUP] = pack(rows)
        others(lambda d, p=p: back_copy(p, d, me).start())
        returned_v[p, me] = back_v[p, me]

    others(lambda d: mass_copy(d, d).wait_recv())
    load_ref[...] = jnp.sum(mass_v[...], axis=0).reshape(EXPERTS_ALL)

    for p in range(pieces):
        others(lambda d, p=p: back_copy(p, d, d).wait_recv())
        mixed = jnp.zeros((segs * tok_rows, seg_w), F32)
        for g in range(groups):
            slabs = returned_v[p, g * GROUP : (g + 1) * GROUP].reshape(slab_rows, seg_w)
            mixed = mixed + dot(mixing_v[g], jnp.concatenate([slabs, slabs], axis=0))
        for s in range(segs):
            low = p * piece_w + s * seg_w
            out_ref[:, low : low + seg_w] = mixed[s * tok_rows : (s + 1) * tok_rows].astype(BF16)

    others(lambda d: mass_copy(d, d).wait_send())
    for p in range(pieces):
        others(lambda d, p=p: token_copy(p, d, d).wait_send())
        others(lambda d, p=p: back_copy(p, d, d).wait_send())


def mixing_lanes(n):
    return -(-n * CAP // 128) * 128


def copy_out(combined_in, load_in, combined_out, load_out, sem):
    copies = [
        pltpu.make_async_copy(combined_in, combined_out, sem.at[0]),
        pltpu.make_async_copy(load_in, load_out, sem.at[1]),
    ]
    for copy in copies:
        copy.start()
    for copy in copies:
        copy.wait()


def shards(tokens, expert_ids, gate_scores, gate_weight, up_weight, down_weight):
    n = lax.axis_size("exp")
    tok_rows, width = tokens.shape
    hid_dev = gate_weight.shape[1]
    spread = FF // hid_dev
    tiles = width // 128
    segs = max(s for s in range(1, SLAB // CAP + 1) if tiles % s == 0)
    pieces = 2 if tiles % (2 * segs) == 0 else 1
    piece_w = width // pieces
    seg_w = piece_w // segs
    groups = n // GROUP
    cfg = (n, spread, segs, pieces, piece_w, seg_w)
    dma = pltpu.SemaphoreType.DMA
    scratch = [
        pltpu.VMEM(tokens.shape, BF16),
        pltpu.VMEM(expert_ids.shape[::-1], jnp.int32),
        pltpu.VMEM(gate_scores.shape[::-1], F32),
        pltpu.VMEM((pieces, piece_w, hid_dev), BF16),
        pltpu.VMEM((pieces, piece_w, hid_dev), BF16),
        pltpu.VMEM((pieces, hid_dev, piece_w), BF16),
        pltpu.VMEM((pieces, n, SLAB, seg_w), BF16),
        pltpu.VMEM((pieces, n, SLAB, seg_w), BF16),
        pltpu.VMEM((pieces, n, SLAB, seg_w), BF16),
        pltpu.VMEM((pieces, n, SLAB, seg_w), BF16),
        pltpu.VMEM((n, 1, EXPERTS_ALL), F32),
        pltpu.VMEM((groups, segs * tok_rows, 2 * GROUP * SLAB), BF16),
        pltpu.VMEM((n * CAP, piece_w), BF16),
        pltpu.VMEM((n * CAP, hid_dev), F32),
        pltpu.VMEM((n * CAP, hid_dev), F32),
        pltpu.VMEM((n * CAP, hid_dev), BF16),
        dma((3,)),
        dma((pieces,)),
        dma((pieces,)),
        dma((pieces,)),
        dma((pieces, n)),
        dma((pieces, n)),
        dma((n,)),
        dma((n,)),
        dma((pieces, n)),
        dma((pieces, n)),
    ]
    anywhere = pl.BlockSpec(memory_space=pl.ANY)
    out_shape = (
        jax.ShapeDtypeStruct(tokens.shape, BF16),
        jax.ShapeDtypeStruct((EXPERTS_ALL,), F32),
    )
    combined, load = pl.pallas_call(
        functools.partial(kernel, cfg),
        out_shape=out_shape,
        in_specs=[pl.BlockSpec(memory_space=pltpu.HBM)] * 6,
        out_specs=(pl.BlockSpec(memory_space=pltpu.VMEM), pl.BlockSpec(memory_space=pltpu.VMEM)),
        scratch_shapes=scratch,
        compiler_params=pltpu.CompilerParams(
            collective_id=0, has_side_effects=True, vmem_limit_bytes=62 * 1024 * 1024
        ),
    )(tokens, expert_ids.T, gate_scores.T, gate_weight, up_weight, down_weight)
    return pl.pallas_call(
        copy_out,
        out_shape=out_shape,
        in_specs=[anywhere] * 2,
        out_specs=(anywhere, anywhere),
        scratch_shapes=[dma((2,))],
    )(combined, load)


def solution(mesh):
    return jax.shard_map(
        shards,
        mesh=mesh,
        in_specs=(
            P(("rep", "exp"), None),
            P(("rep", "exp"), None),
            P(("rep", "exp"), None),
            P(None, "exp"),
            P(None, "exp"),
            P("exp", None),
        ),
        out_specs=(P(("rep", "exp"), None), P("rep")),
        check_vma=False,
    )
```

time: 39.7 us -> 37.5 us (0.945)
  local copies, waits for them, and re-layouts: 4.37 us -> 0 us
  Pallas kernels: 33.2 us -> 36.7 us
  other arithmetic: 1.23 us -> 0 us
    unnamed x3 -> x0, local copies, waits for them, and re-layouts: 4.37 us -> none
    pallas_call x1 -> x2, Pallas kernels: 33.2 us -> 36.7 us  [the longest x1 28.6 us: shards(): pl.pallas_call(functools.partial(kernel, cfg), out_shape=out_shape, in_sp...]
    pallas_call x1 -> x0, other arithmetic: 1.23 us -> none  [shards(): pl.pallas_call(functools.partial(kernel, cfg), out_shape=(jax.ShapeDtypeS...]
where the time goes in v2:
time: 37.5 us; the launch traced here: 37.3 us
  Pallas kernels  36.7 us (98%)
  between operations  0.64 us (2%)
    pallas_call x1, Pallas kernels, shards(): pl.pallas_call(functools.partial(kernel, cfg), out_shape=out_shape, in_sp...  28.6 us
    pallas_call x1, Pallas kernels, shards(): pl.pallas_call(copy_out, out_shape=out_shape, in_specs=[anywhere] * 2, ou...  8.12 us

profile of v2, /device:TPU:0, one launch (start us, length us, event | category | flops | bytes accessed | tf_op | source)
XLA Modules:
  0.0 37.3 jit_solution(1771910507310386029)
XLA Ops:
  0.6 28.6 %shard_map.77 = (bf16[32,3584]{1,0:T(8,128)(2,1)}, f32[384]{0:T(512)}) custom-call(bf16[32,3584]{1,0:T(8,128)(2,1)} %tokens_hbm.1, s32[8,32]{1,0:T(8,128)} %bitcast.2, f32[8,32]{1,0:T(8,128)} %bitcast.3, bf16[3584,2048]{1,0:T(8,128)(2,1)} %gate_hbm.1, bf16[3584,2048]{1,0:T(8,128)(2,1)} %up_hbm.1, bf16[2048,3584]{1,0:T(8,128)(2,1)} %down_hbm.1), custom_call_target="tpu_custom_call" | custom-call | tf_op jit(solution)/shard_map/pallas_call | solution.py:300
  29.2 8.1 %shard_map.78 = (bf16[32,3584]{1,0:T(8,128)(2,1)}, f32[384]{0:T(512)}) custom-call(bf16[32,3584]{1,0:T(8,128)(2,1)} %get-tuple-element.4.combined_in, f32[384]{0:T(512)} %get-tuple-element.5.load_in), custom_call_target="tpu_custom_call" | custom-call | tf_op jit(solution)/shard_map/pallas_call | solution.py:310

commit v3 on v2

--- a/solution.py
+++ b/solution.py
@@ -73,11 +73,8 @@
             down_hbm.at[:, pl.ds(p * piece_w, piece_w)], down_v.at[p], down_sem.at[p]
         )
 
-    for p in range(pieces):
-        gate_copy(p).start()
-        up_copy(p).start()
-    for p in range(pieces):
-        down_copy(p).start()
+    gate_copy(0).start()
+    up_copy(0).start()
 
     def others(body):
         def step(i, carry):
@@ -150,6 +147,11 @@
     for p in range(pieces):
         others(lambda d, p=p: token_copy(p, d, me).start())
         arrived_v[p, me] = send_v[p, me]
+    for p in range(1, pieces):
+        gate_copy(p).start()
+        up_copy(p).start()
+    for p in range(pieces):
+        down_copy(p).start()
     others(lambda d: mass_copy(d, me).start())
 
     weights = jnp.where(placed, gates, 0.0)
@@ -240,15 +242,9 @@
     return -(-n * CAP // 128) * 128
 
 
-def copy_out(combined_in, load_in, combined_out, load_out, sem):
-    copies = [
-        pltpu.make_async_copy(combined_in, combined_out, sem.at[0]),
-        pltpu.make_async_copy(load_in, load_out, sem.at[1]),
-    ]
-    for copy in copies:
-        copy.start()
-    for copy in copies:
-        copy.wait()
+def copy_out(combined_in, load_in, combined_out, load_out):
+    combined_out[...] = combined_in[...]
+    load_out[...] = load_in[...]
 
 
 def shards(tokens, expert_ids, gate_scores, gate_weight, up_weight, down_weight):
@@ -292,7 +288,7 @@
         dma((pieces, n)),
         dma((pieces, n)),
     ]
-    anywhere = pl.BlockSpec(memory_space=pl.ANY)
+    vmem = pl.BlockSpec(memory_space=pltpu.VMEM)
     out_shape = (
         jax.ShapeDtypeStruct(tokens.shape, BF16),
         jax.ShapeDtypeStruct((EXPERTS_ALL,), F32),
@@ -301,7 +297,7 @@
         functools.partial(kernel, cfg),
         out_shape=out_shape,
         in_specs=[pl.BlockSpec(memory_space=pltpu.HBM)] * 6,
-        out_specs=(pl.BlockSpec(memory_space=pltpu.VMEM), pl.BlockSpec(memory_space=pltpu.VMEM)),
+        out_specs=(vmem, vmem),
         scratch_shapes=scratch,
         compiler_params=pltpu.CompilerParams(
             collective_id=0, has_side_effects=True, vmem_limit_bytes=62 * 1024 * 1024
@@ -310,9 +306,8 @@
     return pl.pallas_call(
         copy_out,
         out_shape=out_shape,
-        in_specs=[anywhere] * 2,
-        out_specs=(anywhere, anywhere),
-        scratch_shapes=[dma((2,))],
+        in_specs=[vmem, vmem],
+        out_specs=(vmem, vmem),
     )(combined, load)
 
 

time: 37.5 us -> 28.5 us (0.76)
  Pallas kernels: 36.7 us -> 27.7 us
    pallas_call x1, Pallas kernels: 8.12 us -> 1.65 us  [shards(): pl.pallas_call(copy_out, out_shape=out_shape, in_specs=[vmem, vmem], out_...]
    pallas_call x1, Pallas kernels: 28.6 us -> 26.1 us  [shards(): pl.pallas_call(functools.partial(kernel, cfg), out_shape=out_shape, in_sp...]
where the time goes in v3:
time: 28.5 us; the launch traced here: 28.3 us
  Pallas kernels  27.7 us (97%)
  between operations  0.64 us (2%)
    pallas_call x1, Pallas kernels, shards(): pl.pallas_call(functools.partial(kernel, cfg), out_shape=out_shape, in_sp...  26.1 us
    pallas_call x1, Pallas kernels, shards(): pl.pallas_call(copy_out, out_shape=out_shape, in_specs=[vmem, vmem], out_...  1.65 us

profile of v3, /device:TPU:0, one launch (start us, length us, event | category | flops | bytes accessed | tf_op | source)
XLA Modules:
  0.0 28.3 jit_solution(9400939913194411490)
XLA Ops:
  0.6 26.1 %shard_map.77 = (bf16[32,3584]{1,0:T(8,128)(2,1)}, f32[384]{0:T(512)}) custom-call(bf16[32,3584]{1,0:T(8,128)(2,1)} %tokens_hbm.1, s32[8,32]{1,0:T(8,128)} %bitcast.2, f32[8,32]{1,0:T(8,128)} %bitcast.3, bf16[3584,2048]{1,0:T(8,128)(2,1)} %gate_hbm.1, bf16[3584,2048]{1,0:T(8,128)(2,1)} %up_hbm.1, bf16[2048,3584]{1,0:T(8,128)(2,1)} %down_hbm.1), custom_call_target="tpu_custom_call" | custom-call | tf_op jit(solution)/shard_map/pallas_call | solution.py:296
  26.7 1.6 %shard_map.78 = (bf16[32,3584]{1,0:T(8,128)(2,1)}, f32[384]{0:T(512)}) custom-call(bf16[32,3584]{1,0:T(8,128)(2,1)} %get-tuple-element.4.combined_in, f32[384]{0:T(512)} %get-tuple-element.5.load_in), custom_call_target="tpu_custom_call" | custom-call | tf_op jit(solution)/shard_map/pallas_call | solution.py:306

commit v4 on v3

v4 whole, which is shorter than its diff:
```python
import functools

import jax
import jax.numpy as jnp
from jax import lax
from jax.experimental import pallas as pl
from jax.experimental.pallas import tpu as pltpu
from jax.sharding import PartitionSpec as P

FF = 2048
EXPERTS_ALL = 384
CAP = 2
SLAB = 16
GROUP = 8
SEGS = SLAB // CAP
LANES = 128
TILE = 256
MESH = pl.DeviceIdType.MESH
BF16 = jnp.bfloat16
F32 = jnp.float32


def dot(a, b):
    return jnp.dot(a, b, preferred_element_type=F32)


def iota(shape, dim):
    return lax.broadcasted_iota(jnp.int32, shape, dim)


def one_hot(mask):
    return jnp.where(mask, 1.0, 0.0).astype(BF16)


def slab_place(i):
    dev, seg, row = i // SLAB, (i % SLAB) // CAP, i % CAP
    return seg * (GROUP * CAP) + dev * CAP + row


def cut(width):
    pieces, low, lane = [], 0, 0
    while low < width:
        seg_w = 2 * LANES if width - low >= 2 * LANES * SEGS else LANES
        segs = min(SEGS, (width - low) // seg_w)
        pieces.append((low, lane, segs, seg_w))
        low, lane = low + segs * seg_w, lane + seg_w
    return pieces


def kernel(
    cfg,
    tokens_hbm, ids_hbm, scores_hbm, gate_hbm, up_hbm, down_hbm,
    returned_hbm, mixing_hbm, load_hbm,
    tokens_v, ids_v, scores_v, gate_v, up_v, down_v,
    send_v, arrived_v, back_v, mass_v, load_v, mixing_v, x_v, gate_sum, up_sum, hidden_v,
    small_sem, gate_sem, up_sem, down_sem, out_sem, own_sem,
    send_sem, recv_sem, mass_send_sem, mass_recv_sem, back_send_sem, back_recv_sem,
):
    n, spread, pieces = cfg
    groups = n // GROUP
    top, tok_rows = ids_v.shape
    lanes = mixing_lanes(n)
    me = lax.axis_index("exp")
    forward = list(enumerate(pieces))
    backward = forward[::-1]

    small = [
        pltpu.make_async_copy(ids_hbm, ids_v, small_sem.at[0]),
        pltpu.make_async_copy(scores_hbm, scores_v, small_sem.at[1]),
        pltpu.make_async_copy(tokens_hbm, tokens_v, small_sem.at[2]),
    ]
    for copy in small:
        copy.start()

    def columns(piece):
        low, _, segs, seg_w = piece
        return pl.ds(low, segs * seg_w)

    def gate_copy(p):
        rows = columns(pieces[p])
        return pltpu.make_async_copy(gate_hbm.at[rows, :], gate_v.at[rows, :], gate_sem.at[p])

    def up_copy(p):
        rows = columns(pieces[p])
        return pltpu.make_async_copy(up_hbm.at[rows, :], up_v.at[rows, :], up_sem.at[p])

    def down_copy(p):
        cols = columns(pieces[p])
        return pltpu.make_async_copy(down_hbm.at[:, cols], down_v.at[:, cols], down_sem.at[p])

    for p, _ in backward[:-1]:
        gate_copy(p).start()
        up_copy(p).start()

    def others(body):
        def step(i, carry):
            body(lax.rem(me + i, n))
            return carry

        lax.fori_loop(1, n, step, 0, unroll=n <= 16)

    barrier = pltpu.get_barrier_semaphore()
    others(lambda d: pl.semaphore_signal(barrier, inc=1, device_id={"exp": d}, device_id_type=MESH))

    for copy in small[:2]:
        copy.wait()
    ids = jnp.transpose(ids_v[...])
    scores = jnp.transpose(scores_v[...])
    all_ids = iota((tok_rows, EXPERTS_ALL), 1)
    slot = iota((tok_rows, lanes), 1)
    slot_expert = jnp.where(slot < n * CAP, slot // (CAP * spread), -1)
    mass = jnp.zeros((tok_rows, EXPERTS_ALL), F32)
    gates = jnp.zeros((tok_rows, lanes), F32)
    hits = jnp.zeros((tok_rows, lanes), F32)
    for k in range(top):
        id_k, score_k = ids[:, k : k + 1], scores[:, k : k + 1]
        mass = mass + jnp.where(id_k == all_ids, score_k, 0.0)
        found = id_k == slot_expert
        gates = gates + jnp.where(found, score_k, 0.0)
        hits = hits + jnp.where(found, 1.0, 0.0)
    earlier = one_hot(iota((tok_rows, tok_rows), 1) < iota((tok_rows, tok_rows), 0))
    position = dot(earlier, hits.astype(BF16))
    placed = (hits > 0.5) & (position == (slot % CAP).astype(F32))
    picker = jnp.transpose(jnp.where(placed, 1.0, 0.0)).astype(BF16)
    mass_v[me] = jnp.sum(mass, axis=0, keepdims=True)

    slab_rows = GROUP * SLAB
    square = (slab_rows, slab_rows)
    to_slab = one_hot(slab_place(iota(square, 0)) == iota(square, 1))
    from_slab = one_hot(slab_place(iota(square, 1)) == iota(square, 0))

    def pack(rows, piece):
        _, _, segs, seg_w = piece
        parts = [rows[:, s * seg_w : (s + 1) * seg_w] for s in range(segs)]
        parts += [jnp.zeros_like(parts[0])] * (SEGS - segs)
        packed = jnp.concatenate(parts, axis=0)
        return dot(to_slab, packed).astype(BF16).reshape(GROUP, SLAB, seg_w)

    def slab_lanes(piece):
        return slice(piece[1], piece[1] + piece[3])

    small[2].wait()
    tokens = tokens_v[...]
    for g in range(groups):
        rows = picker[g * GROUP * CAP : (g + 1) * GROUP * CAP]
        picked = dot(rows, tokens).astype(BF16)
        for p, piece in backward:
            low, _, segs, seg_w = piece
            send_v[g * GROUP : (g + 1) * GROUP, :, slab_lanes(piece)] = pack(
                picked[:, low : low + segs * seg_w], piece
            )

    def token_copy(p, d, src):
        at = pl.ds(pieces[p][1], pieces[p][3])
        return pltpu.make_async_remote_copy(
            src_ref=send_v.at[d, :, at], dst_ref=arrived_v.at[src, :, at],
            send_sem=send_sem.at[p, d], recv_sem=recv_sem.at[p, src],
            device_id={"exp": d}, device_id_type=MESH,
        )

    def mass_copy(d, src):
        return pltpu.make_async_remote_copy(
            src_ref=mass_v.at[me], dst_ref=mass_v.at[src],
            send_sem=mass_send_sem.at[d], recv_sem=mass_recv_sem.at[src],
            device_id={"exp": d}, device_id_type=MESH,
        )

    pl.semaphore_wait(barrier, n - 1)
    for p, _ in backward:
        others(lambda d, p=p: token_copy(p, d, me).start())
    arrived_v[me] = send_v[me]
    gate_copy(0).start()
    up_copy(0).start()
    for p, _ in forward:
        down_copy(p).start()
    others(lambda d: mass_copy(d, me).start())

    weights = jnp.where(placed, gates, 0.0)
    weights_hi = weights.astype(BF16)
    weights_lo = (weights - weights_hi.astype(F32)).astype(BF16)
    slab_lane = iota((lanes, slab_rows), 1)
    lane_seg = (iota((tok_rows, slab_rows), 1) % SLAB) // CAP
    for g in range(groups):
        slot_of = g * GROUP * CAP + slab_lane // SLAB * CAP + slab_lane % CAP
        spreading = one_hot(iota((lanes, slab_rows), 0) == slot_of)
        for part, term in enumerate((weights_hi, weights_lo)):
            wide = dot(term, spreading)
            for s in range(SEGS):
                mixing_v[
                    g, s * tok_rows : (s + 1) * tok_rows, part * slab_rows : (part + 1) * slab_rows
                ] = jnp.where(lane_seg == s, wide, 0.0).astype(BF16)

    mixing_out = pltpu.make_async_copy(mixing_v, mixing_hbm, out_sem.at[0])
    mixing_out.start()

    hid_dev = hidden_v.shape[1]
    hid_tile = min(TILE, hid_dev)
    for p, piece in backward:
        low, _, segs, seg_w = piece
        at = slice(low, low + segs * seg_w)
        others(lambda d, p=p: token_copy(p, d, d).wait_recv())
        for g in range(groups):
            slabs = arrived_v[g * GROUP : (g + 1) * GROUP, :, slab_lanes(piece)]
            packed = dot(from_slab, slabs.reshape(slab_rows, seg_w)).astype(BF16)
            size = GROUP * CAP
            for s in range(segs):
                x_v[g * size : (g + 1) * size, low + s * seg_w : low + (s + 1) * seg_w] = packed[
                    s * size : (s + 1) * size
                ]
        gate_copy(p).wait()
        up_copy(p).wait()

        def gate_up(j, carry, p=p, at=at):
            cols = pl.ds(pl.multiple_of(j * hid_tile, hid_tile), hid_tile)
            gate_act = dot(x_v[:, at], gate_v[at, cols])
            up_act = dot(x_v[:, at], up_v[at, cols])
            if p < len(pieces) - 1:
                gate_act = gate_act + gate_sum[:, cols]
                up_act = up_act + up_sum[:, cols]
            if p > 0:
                gate_sum[:, cols] = gate_act
                up_sum[:, cols] = up_act
            else:
                silu = gate_act / (1.0 + jnp.exp(-gate_act))
                hidden_v[:, cols] = (silu * up_act).astype(BF16)
            return carry

        lax.fori_loop(0, hid_dev // hid_tile, gate_up, 0, unroll=2 if hid_dev > hid_tile else 1)

    others(lambda d: mass_copy(d, d).wait_recv())
    load_v[...] = jnp.sum(mass_v[...], axis=0)
    load_out = pltpu.make_async_copy(load_v, load_hbm, out_sem.at[1])
    load_out.start()

    def back_copy(p, d, src):
        at = pl.ds(pieces[p][1], pieces[p][3])
        return pltpu.make_async_remote_copy(
            src_ref=back_v.at[d, :, at], dst_ref=returned_hbm.at[src, :, at],
            send_sem=back_send_sem.at[p, d], recv_sem=back_recv_sem.at[p, src],
            device_id={"exp": d}, device_id_type=MESH,
        )

    def own_copy(p):
        at = pl.ds(pieces[p][1], pieces[p][3])
        return pltpu.make_async_copy(
            back_v.at[me, :, at], returned_hbm.at[me, :, at], own_sem.at[p]
        )

    for p, piece in forward:
        low, _, segs, seg_w = piece
        down_copy(p).wait()
        tile = min(TILE, segs * seg_w)
        for first in range(low, low + segs * seg_w, tile):
            cols = slice(first, first + tile)
            x_v[:, cols] = dot(hidden_v[...], down_v[:, cols]).astype(BF16)
        for g in range(groups):
            rows = x_v[g * GROUP * CAP : (g + 1) * GROUP * CAP, low : low + segs * seg_w]
            back_v[g * GROUP : (g + 1) * GROUP, :, slab_lanes(piece)] = pack(rows, piece)
        others(lambda d, p=p: back_copy(p, d, me).start())
        own_copy(p).start()

    mixing_out.wait()
    load_out.wait()
    others(lambda d: mass_copy(d, d).wait_send())
    for p, _ in forward:
        others(lambda d, p=p: token_copy(p, d, d).wait_send())
        others(lambda d, p=p: back_copy(p, d, d).wait_send())
        own_copy(p).wait()
    for p, _ in forward:
        others(lambda d, p=p: back_copy(p, d, d).wait_recv())


def mixing_lanes(n):
    return -(-n * CAP // 128) * 128


def combine(pieces, returned_ref, mixing_ref, load_in, out_ref, load_out):
    tok_rows = out_ref.shape[0]
    groups, _, depth = mixing_ref.shape
    for low, lane, segs, seg_w in pieces:
        mixed = jnp.zeros((segs * tok_rows, seg_w), F32)
        for g in range(groups):
            slabs = returned_ref[g * GROUP : (g + 1) * GROUP, :, lane : lane + seg_w]
            slabs = slabs.reshape(depth // 2, seg_w)
            mixing = mixing_ref[g, : segs * tok_rows, :]
            mixed = mixed + dot(mixing, jnp.concatenate([slabs, slabs], axis=0))
        for s in range(segs):
            out_ref[:, low + s * seg_w : low + (s + 1) * seg_w] = mixed[
                s * tok_rows : (s + 1) * tok_rows
            ].astype(BF16)
    load_out[...] = load_in[...].reshape(EXPERTS_ALL)


def shards(tokens, expert_ids, gate_scores, gate_weight, up_weight, down_weight):
    n = lax.axis_size("exp")
    tok_rows, width = tokens.shape
    hid_dev = gate_weight.shape[1]
    spread = FF // hid_dev
    pieces = cut(width)
    count = len(pieces)
    slab_w = pieces[-1][1] + pieces[-1][3]
    groups = n // GROUP
    cfg = (n, spread, pieces)
    dma = pltpu.SemaphoreType.DMA
    slabs = (n, SLAB, slab_w)
    mixing = (groups, SEGS * tok_rows, 2 * GROUP * SLAB)
    scratch = [
        pltpu.VMEM(tokens.shape, BF16),
        pltpu.VMEM(expert_ids.shape[::-1], jnp.int32),
        pltpu.VMEM(gate_scores.shape[::-1], F32),
        pltpu.VMEM(gate_weight.shape, BF16),
        pltpu.VMEM(up_weight.shape, BF16),
        pltpu.VMEM(down_weight.shape, BF16),
        pltpu.VMEM(slabs, BF16),
        pltpu.VMEM(slabs, BF16),
        pltpu.VMEM(slabs, BF16),
        pltpu.VMEM((n, 1, EXPERTS_ALL), F32),
        pltpu.VMEM((1, EXPERTS_ALL), F32),
        pltpu.VMEM(mixing, BF16),
        pltpu.VMEM((n * CAP, width), BF16),
        pltpu.VMEM((n * CAP, hid_dev), F32),
        pltpu.VMEM((n * CAP, hid_dev), F32),
        pltpu.VMEM((n * CAP, hid_dev), BF16),
        dma((3,)),
        dma((count,)),
        dma((count,)),
        dma((count,)),
        dma((2,)),
        dma((count,)),
        dma((count, n)),
        dma((count, n)),
        dma((n,)),
        dma((n,)),
        dma((count, n)),
        dma((count, n)),
    ]
    vmem = pl.BlockSpec(memory_space=pltpu.VMEM)
    hbm = pl.BlockSpec(memory_space=pltpu.HBM)
    partials = pl.pallas_call(
        functools.partial(kernel, cfg),
        out_shape=(
            jax.ShapeDtypeStruct(slabs, BF16),
            jax.ShapeDtypeStruct(mixing, BF16),
            jax.ShapeDtypeStruct((1, EXPERTS_ALL), F32),
        ),
        in_specs=[hbm] * 6,
        out_specs=(hbm, hbm, hbm),
        scratch_shapes=scratch,
        compiler_params=pltpu.CompilerParams(
            collective_id=0, has_side_effects=True, vmem_limit_bytes=62 * 1024 * 1024
        ),
    )(tokens, expert_ids.T, gate_scores.T, gate_weight, up_weight, down_weight)
    return pl.pallas_call(
        functools.partial(combine, pieces),
        out_shape=(
            jax.ShapeDtypeStruct(tokens.shape, BF16),
            jax.ShapeDtypeStruct((EXPERTS_ALL,), F32),
        ),
        in_specs=[vmem] * 3,
        out_specs=(vmem, vmem),
    )(*partials)


def solution(mesh):
    return jax.shard_map(
        shards,
        mesh=mesh,
        in_specs=(
            P(("rep", "exp"), None),
            P(("rep", "exp"), None),
            P(("rep", "exp"), None),
            P(None, "exp"),
            P(None, "exp"),
            P("exp", None),
        ),
        out_specs=(P(("rep", "exp"), None), P("rep")),
        check_vma=False,
    )
```

time: 28.5 us -> 30.2 us (1.060)
  Pallas kernels: 27.7 us -> 29.4 us
    pallas_call x2, Pallas kernels: 27.7 us -> 29.4 us  [the longest x1 27.5 us: shards(): pl.pallas_call(functools.partial(kernel, cfg), out_shape=(jax.ShapeDtypeS...]
where the time goes in v4:
time: 30.2 us; the launch traced here: 30 us
  Pallas kernels  29.4 us (97%)
  between operations  0.64 us (2%)
    pallas_call x1, Pallas kernels, shards(): pl.pallas_call(functools.partial(kernel, cfg), out_shape=(jax.ShapeDtypeS...  27.5 us
    pallas_call x1, Pallas kernels, shards(): pl.pallas_call(functools.partial(combine, pieces), out_shape=(jax.ShapeDt...  1.89 us

profile of v4, /device:TPU:0, one launch (start us, length us, event | category | flops | bytes accessed | tf_op | source)
XLA Modules:
  0.0 30.0 jit_solution(12415733224257324285)
XLA Ops:
  0.6 27.5 %shard_map.77 = (bf16[8,16,512]{2,1,0:T(8,128)(2,1)}, bf16[1,256,256]{2,1,0:T(8,128)(2,1)}, f32[1,384]{1,0:T(1,128)}) custom-call(bf16[32,3584]{1,0:T(8,128)(2,1)} %tokens_hbm.1, s32[8,32]{1,0:T(8,128)} %bitcast.2, f32[8,32]{1,0:T(8,128)} %bitcast.3, bf16[3584,2048]{1,0:T(8,128)(2,1)} %gate_hbm.1, bf16[3584,2048]{1,0:T(8,128)(2,1)} %up_hbm.1, ...), custom_call_target="tpu_custom_call" | custom-call | tf_op jit(solution)/shard_map/pallas_call | solution.py:339
  28.1 1.9 %shard_map.78 = (bf16[32,3584]{1,0:T(8,128)(2,1)}, f32[384]{0:T(512)}) custom-call(bf16[8,16,512]{2,1,0:T(8,128)(2,1)} %get-tuple-element.5.returned_ref, bf16[1,256,256]{2,1,0:T(8,128)(2,1)} %get-tuple-element.6.mixing_ref, f32[1,384]{1,0:T(1,128)} %get-tuple-element.7.load_in), custom_call_target="tpu_custom_call" | custom-call | tf_op jit(solution)/shard_map/pallas_call | solution.py:353

commit v5 on v4

--- a/solution.py
+++ b/solution.py
@@ -15,6 +15,7 @@
 SEGS = SLAB // CAP
 LANES = 128
 TILE = 256
+BLOCK = 512
 MESH = pl.DeviceIdType.MESH
 BF16 = jnp.bfloat16
 F32 = jnp.float32
@@ -39,12 +40,16 @@
 
 def cut(width):
     pieces, low, lane = [], 0, 0
+    seg_w = 2 * LANES if width % (2 * LANES) == 0 else LANES
     while low < width:
-        seg_w = 2 * LANES if width - low >= 2 * LANES * SEGS else LANES
         segs = min(SEGS, (width - low) // seg_w)
         pieces.append((low, lane, segs, seg_w))
         low, lane = low + segs * seg_w, lane + seg_w
     return pieces
+
+
+def blocks(first, size):
+    return [pl.ds(low, min(BLOCK, first + size - low)) for low in range(first, first + size, BLOCK)]
 
 
 def kernel(
@@ -76,21 +81,29 @@
         low, _, segs, seg_w = piece
         return pl.ds(low, segs * seg_w)
 
-    def gate_copy(p):
-        rows = columns(pieces[p])
-        return pltpu.make_async_copy(gate_hbm.at[rows, :], gate_v.at[rows, :], gate_sem.at[p])
-
-    def up_copy(p):
-        rows = columns(pieces[p])
-        return pltpu.make_async_copy(up_hbm.at[rows, :], up_v.at[rows, :], up_sem.at[p])
-
-    def down_copy(p):
+    def gate_up_copies(p):
+        low, _, segs, seg_w = pieces[p]
+        copies = []
+        for i, rows in enumerate(blocks(low, segs * seg_w)):
+            copies += [
+                pltpu.make_async_copy(gate_hbm.at[rows, :], gate_v.at[rows, :], gate_sem.at[p, i]),
+                pltpu.make_async_copy(up_hbm.at[rows, :], up_v.at[rows, :], up_sem.at[p, i]),
+            ]
+        return copies
+
+    def down_copies(p):
         cols = columns(pieces[p])
-        return pltpu.make_async_copy(down_hbm.at[:, cols], down_v.at[:, cols], down_sem.at[p])
-
-    for p, _ in backward[:-1]:
-        gate_copy(p).start()
-        up_copy(p).start()
+        return [
+            pltpu.make_async_copy(down_hbm.at[rows, cols], down_v.at[rows, cols], down_sem.at[p, i])
+            for i, rows in enumerate(blocks(0, down_hbm.shape[0]))
+        ]
+
+    for p, _ in backward:
+        for copy in gate_up_copies(p):
+            copy.start(priority=1)
+    for p, _ in forward:
+        for copy in down_copies(p):
+            copy.start(priority=1)
 
     def others(body):
         def step(i, carry):
@@ -169,10 +182,6 @@
     for p, _ in backward:
         others(lambda d, p=p: token_copy(p, d, me).start())
     arrived_v[me] = send_v[me]
-    gate_copy(0).start()
-    up_copy(0).start()
-    for p, _ in forward:
-        down_copy(p).start()
     others(lambda d: mass_copy(d, me).start())
 
     weights = jnp.where(placed, gates, 0.0)
@@ -207,8 +216,8 @@
                 x_v[g * size : (g + 1) * size, low + s * seg_w : low + (s + 1) * seg_w] = packed[
                     s * size : (s + 1) * size
                 ]
-        gate_copy(p).wait()
-        up_copy(p).wait()
+        for copy in gate_up_copies(p):
+            copy.wait()
 
         def gate_up(j, carry, p=p, at=at):
             cols = pl.ds(pl.multiple_of(j * hid_tile, hid_tile), hid_tile)
@@ -248,7 +257,8 @@
 
     for p, piece in forward:
         low, _, segs, seg_w = piece
-        down_copy(p).wait()
+        for copy in down_copies(p):
+            copy.wait()
         tile = min(TILE, segs * seg_w)
         for first in range(low, low + segs * seg_w, tile):
             cols = slice(first, first + tile)
@@ -322,9 +332,9 @@
         pltpu.VMEM((n * CAP, hid_dev), F32),
         pltpu.VMEM((n * CAP, hid_dev), BF16),
         dma((3,)),
-        dma((count,)),
-        dma((count,)),
-        dma((count,)),
+        dma((count, -(-width // BLOCK))),
+        dma((count, -(-width // BLOCK))),
+        dma((count, -(-hid_dev // BLOCK))),
         dma((2,)),
         dma((count,)),
         dma((count, n)),

time: 30.2 us -> 29.2 us (0.967)
  Pallas kernels: 29.4 us -> 28.4 us
    pallas_call x1, Pallas kernels: 27.5 us -> 26.5 us  [shards(): pl.pallas_call(functools.partial(kernel, cfg), out_shape=(jax.ShapeDtypeS...]
where the time goes in v5:
time: 29.2 us; the launch traced here: 29 us
  Pallas kernels  28.4 us (97%)
  between operations  0.64 us (2%)
    pallas_call x1, Pallas kernels, shards(): pl.pallas_call(functools.partial(kernel, cfg), out_shape=(jax.ShapeDtypeS...  26.5 us
    pallas_call x1, Pallas kernels, shards(): pl.pallas_call(functools.partial(combine, pieces), out_shape=(jax.ShapeDt...  1.89 us

profile of v5, /device:TPU:0, one launch (start us, length us, event | category | flops | bytes accessed | tf_op | source)
XLA Modules:
  0.0 29.0 jit_solution(13833207931528477762)
XLA Ops:
  0.6 26.5 %shard_map.77 = (bf16[8,16,512]{2,1,0:T(8,128)(2,1)}, bf16[1,256,256]{2,1,0:T(8,128)(2,1)}, f32[1,384]{1,0:T(1,128)}) custom-call(bf16[32,3584]{1,0:T(8,128)(2,1)} %tokens_hbm.1, s32[8,32]{1,0:T(8,128)} %bitcast.2, f32[8,32]{1,0:T(8,128)} %bitcast.3, bf16[3584,2048]{1,0:T(8,128)(2,1)} %gate_hbm.1, bf16[3584,2048]{1,0:T(8,128)(2,1)} %up_hbm.1, ...), custom_call_target="tpu_custom_call" | custom-call | tf_op jit(solution)/shard_map/pallas_call | solution.py:349
  27.2 1.9 %shard_map.78 = (bf16[32,3584]{1,0:T(8,128)(2,1)}, f32[384]{0:T(512)}) custom-call(bf16[8,16,512]{2,1,0:T(8,128)(2,1)} %get-tuple-element.5.returned_ref, bf16[1,256,256]{2,1,0:T(8,128)(2,1)} %get-tuple-element.6.mixing_ref, f32[1,384]{1,0:T(1,128)} %get-tuple-element.7.load_in), custom_call_target="tpu_custom_call" | custom-call | tf_op jit(solution)/shard_map/pallas_call | solution.py:363

commit v6 on v5

--- a/solution.py
+++ b/solution.py
@@ -14,7 +14,7 @@
 GROUP = 8
 SEGS = SLAB // CAP
 LANES = 128
-TILE = 256
+TILE = 512
 BLOCK = 512
 MESH = pl.DeviceIdType.MESH
 BF16 = jnp.bfloat16
@@ -64,7 +64,6 @@
     n, spread, pieces = cfg
     groups = n // GROUP
     top, tok_rows = ids_v.shape
-    lanes = mixing_lanes(n)
     me = lax.axis_index("exp")
     forward = list(enumerate(pieces))
     backward = forward[::-1]
@@ -115,27 +114,16 @@
     barrier = pltpu.get_barrier_semaphore()
     others(lambda d: pl.semaphore_signal(barrier, inc=1, device_id={"exp": d}, device_id_type=MESH))
 
-    for copy in small[:2]:
-        copy.wait()
-    ids = jnp.transpose(ids_v[...])
-    scores = jnp.transpose(scores_v[...])
-    all_ids = iota((tok_rows, EXPERTS_ALL), 1)
-    slot = iota((tok_rows, lanes), 1)
-    slot_expert = jnp.where(slot < n * CAP, slot // (CAP * spread), -1)
-    mass = jnp.zeros((tok_rows, EXPERTS_ALL), F32)
-    gates = jnp.zeros((tok_rows, lanes), F32)
-    hits = jnp.zeros((tok_rows, lanes), F32)
+    small[0].wait()
+    slots = (n * CAP, tok_rows)
+    slot_expert = iota(slots, 0) // (CAP * spread)
+    hits = jnp.zeros(slots, F32)
     for k in range(top):
-        id_k, score_k = ids[:, k : k + 1], scores[:, k : k + 1]
-        mass = mass + jnp.where(id_k == all_ids, score_k, 0.0)
-        found = id_k == slot_expert
-        gates = gates + jnp.where(found, score_k, 0.0)
-        hits = hits + jnp.where(found, 1.0, 0.0)
-    earlier = one_hot(iota((tok_rows, tok_rows), 1) < iota((tok_rows, tok_rows), 0))
-    position = dot(earlier, hits.astype(BF16))
-    placed = (hits > 0.5) & (position == (slot % CAP).astype(F32))
-    picker = jnp.transpose(jnp.where(placed, 1.0, 0.0)).astype(BF16)
-    mass_v[me] = jnp.sum(mass, axis=0, keepdims=True)
+        hits = hits + jnp.where(ids_v[k : k + 1, :] == slot_expert, 1.0, 0.0)
+    earlier = one_hot(iota((tok_rows, tok_rows), 0) < iota((tok_rows, tok_rows), 1))
+    position = dot(hits.astype(BF16), earlier)
+    placed = (hits > 0.5) & (position == (iota(slots, 0) % CAP).astype(F32))
+    picker = one_hot(placed)
 
     slab_rows = GROUP * SLAB
     square = (slab_rows, slab_rows)
@@ -182,23 +170,37 @@
     for p, _ in backward:
         others(lambda d, p=p: token_copy(p, d, me).start())
     arrived_v[me] = send_v[me]
+
+    small[1].wait()
+    ids = jnp.transpose(ids_v[...])
+    scores = jnp.transpose(scores_v[...])
+    all_ids = iota((tok_rows, EXPERTS_ALL), 1)
+    mass = jnp.zeros((tok_rows, EXPERTS_ALL), F32)
+    for k in range(top):
+        mass = mass + jnp.where(ids[:, k : k + 1] == all_ids, scores[:, k : k + 1], 0.0)
+    mass_v[me] = jnp.sum(mass, axis=0, keepdims=True)
     others(lambda d: mass_copy(d, me).start())
 
+    gates = jnp.zeros(slots, F32)
+    for k in range(top):
+        found = ids_v[k : k + 1, :] == slot_expert
+        gates = gates + jnp.where(found, scores_v[k : k + 1, :], 0.0)
     weights = jnp.where(placed, gates, 0.0)
     weights_hi = weights.astype(BF16)
     weights_lo = (weights - weights_hi.astype(F32)).astype(BF16)
-    slab_lane = iota((lanes, slab_rows), 1)
+    slab_lane = iota((n * CAP, slab_rows), 1)
     lane_seg = (iota((tok_rows, slab_rows), 1) % SLAB) // CAP
     for g in range(groups):
         slot_of = g * GROUP * CAP + slab_lane // SLAB * CAP + slab_lane % CAP
-        spreading = one_hot(iota((lanes, slab_rows), 0) == slot_of)
+        spreading = one_hot(iota((n * CAP, slab_rows), 0) == slot_of)
         for part, term in enumerate((weights_hi, weights_lo)):
-            wide = dot(term, spreading)
+            wide = lax.dot_general(
+                term, spreading, (((0,), (0,)), ((), ())), preferred_element_type=F32
+            )
             for s in range(SEGS):
                 mixing_v[
                     g, s * tok_rows : (s + 1) * tok_rows, part * slab_rows : (part + 1) * slab_rows
                 ] = jnp.where(lane_seg == s, wide, 0.0).astype(BF16)
-
     mixing_out = pltpu.make_async_copy(mixing_v, mixing_hbm, out_sem.at[0])
     mixing_out.start()
 
@@ -234,7 +236,7 @@
                 hidden_v[:, cols] = (silu * up_act).astype(BF16)
             return carry
 
-        lax.fori_loop(0, hid_dev // hid_tile, gate_up, 0, unroll=2 if hid_dev > hid_tile else 1)
+        lax.fori_loop(0, hid_dev // hid_tile, gate_up, 0)
 
     others(lambda d: mass_copy(d, d).wait_recv())
     load_v[...] = jnp.sum(mass_v[...], axis=0)
@@ -278,10 +280,6 @@
         own_copy(p).wait()
     for p, _ in forward:
         others(lambda d, p=p: back_copy(p, d, d).wait_recv())
-
-
-def mixing_lanes(n):
-    return -(-n * CAP // 128) * 128
 
 
 def combine(pieces, returned_ref, mixing_ref, load_in, out_ref, load_out):

time: 29.2 us -> 29.1 us (level)
  no operation moved by 1% of the time
where the time goes in v6:
time: 29.1 us; the launch traced here: 28.9 us
  Pallas kernels  28.3 us (97%)
  between operations  0.64 us (2%)
    pallas_call x1, Pallas kernels, shards(): pl.pallas_call(functools.partial(kernel, cfg), out_shape=(jax.ShapeDtypeS...  26.4 us
    pallas_call x1, Pallas kernels, shards(): pl.pallas_call(functools.partial(combine, pieces), out_shape=(jax.ShapeDt...  1.88 us

profile of v6, /device:TPU:0, one launch (start us, length us, event | category | flops | bytes accessed | tf_op | source)
XLA Modules:
  0.0 28.9 jit_solution(2505515671934347703)
XLA Ops:
  0.6 26.4 %shard_map.77 = (bf16[8,16,512]{2,1,0:T(8,128)(2,1)}, bf16[1,256,256]{2,1,0:T(8,128)(2,1)}, f32[1,384]{1,0:T(1,128)}) custom-call(bf16[32,3584]{1,0:T(8,128)(2,1)} %tokens_hbm.1, s32[8,32]{1,0:T(8,128)} %bitcast.2, f32[8,32]{1,0:T(8,128)} %bitcast.3, bf16[3584,2048]{1,0:T(8,128)(2,1)} %gate_hbm.1, bf16[3584,2048]{1,0:T(8,128)(2,1)} %up_hbm.1, ...), custom_call_target="tpu_custom_call" | custom-call | tf_op jit(solution)/shard_map/pallas_call | solution.py:347
  27.0 1.9 %shard_map.78 = (bf16[32,3584]{1,0:T(8,128)(2,1)}, f32[384]{0:T(512)}) custom-call(bf16[8,16,512]{2,1,0:T(8,128)(2,1)} %get-tuple-element.5.returned_ref, bf16[1,256,256]{2,1,0:T(8,128)(2,1)} %get-tuple-element.6.mixing_ref, f32[1,384]{1,0:T(1,128)} %get-tuple-element.7.load_in), custom_call_target="tpu_custom_call" | custom-call | tf_op jit(solution)/shard_map/pallas_call | solution.py:361

commit v7 on v6

--- a/solution.py
+++ b/solution.py
@@ -38,10 +38,11 @@
     return seg * (GROUP * CAP) + dev * CAP + row
 
 
-def cut(width):
+def cut(width, fine):
     pieces, low, lane = [], 0, 0
-    seg_w = 2 * LANES if width % (2 * LANES) == 0 else LANES
+    wide = 2 * LANES if width % (2 * LANES) == 0 else LANES
     while low < width:
+        seg_w = LANES if fine and width - low < wide * SEGS else wide
         segs = min(SEGS, (width - low) // seg_w)
         pieces.append((low, lane, segs, seg_w))
         low, lane = low + segs * seg_w, lane + seg_w
@@ -55,18 +56,18 @@
 def kernel(
     cfg,
     tokens_hbm, ids_hbm, scores_hbm, gate_hbm, up_hbm, down_hbm,
-    returned_hbm, mixing_hbm, load_hbm,
+    out_ref, load_ref,
     tokens_v, ids_v, scores_v, gate_v, up_v, down_v,
-    send_v, arrived_v, back_v, mass_v, load_v, mixing_v, x_v, gate_sum, up_sum, hidden_v,
-    small_sem, gate_sem, up_sem, down_sem, out_sem, own_sem,
+    send_v, arrived_v, back_v, returned_v, mass_v, mixing_v, x_v, gate_sum, up_sum, hidden_v,
+    small_sem, gate_sem, up_sem, down_sem,
     send_sem, recv_sem, mass_send_sem, mass_recv_sem, back_send_sem, back_recv_sem,
 ):
-    n, spread, pieces = cfg
+    n, spread, pieces, back_pieces = cfg
     groups = n // GROUP
     top, tok_rows = ids_v.shape
     me = lax.axis_index("exp")
-    forward = list(enumerate(pieces))
-    backward = forward[::-1]
+    forward = list(enumerate(back_pieces))
+    backward = list(enumerate(pieces))[::-1]
 
     small = [
         pltpu.make_async_copy(ids_hbm, ids_v, small_sem.at[0]),
@@ -91,18 +92,14 @@
         return copies
 
     def down_copies(p):
-        cols = columns(pieces[p])
+        cols = columns(back_pieces[p])
         return [
             pltpu.make_async_copy(down_hbm.at[rows, cols], down_v.at[rows, cols], down_sem.at[p, i])
             for i, rows in enumerate(blocks(0, down_hbm.shape[0]))
         ]
 
-    for p, _ in backward:
-        for copy in gate_up_copies(p):
-            copy.start(priority=1)
-    for p, _ in forward:
-        for copy in down_copies(p):
-            copy.start(priority=1)
+    for copy in gate_up_copies(backward[0][0]):
+        copy.start()
 
     def others(body):
         def step(i, carry):
@@ -169,6 +166,12 @@
     pl.semaphore_wait(barrier, n - 1)
     for p, _ in backward:
         others(lambda d, p=p: token_copy(p, d, me).start())
+    for p, _ in backward[1:]:
+        for copy in gate_up_copies(p):
+            copy.start()
+    for p, _ in forward:
+        for copy in down_copies(p):
+            copy.start()
     arrived_v[me] = send_v[me]
 
     small[1].wait()
@@ -201,8 +204,6 @@
                 mixing_v[
                     g, s * tok_rows : (s + 1) * tok_rows, part * slab_rows : (part + 1) * slab_rows
                 ] = jnp.where(lane_seg == s, wide, 0.0).astype(BF16)
-    mixing_out = pltpu.make_async_copy(mixing_v, mixing_hbm, out_sem.at[0])
-    mixing_out.start()
 
     hid_dev = hidden_v.shape[1]
     hid_tile = min(TILE, hid_dev)
@@ -239,22 +240,14 @@
         lax.fori_loop(0, hid_dev // hid_tile, gate_up, 0)
 
     others(lambda d: mass_copy(d, d).wait_recv())
-    load_v[...] = jnp.sum(mass_v[...], axis=0)
-    load_out = pltpu.make_async_copy(load_v, load_hbm, out_sem.at[1])
-    load_out.start()
+    load_ref[...] = jnp.sum(mass_v[...], axis=0).reshape(EXPERTS_ALL)
 
     def back_copy(p, d, src):
-        at = pl.ds(pieces[p][1], pieces[p][3])
+        at = pl.ds(back_pieces[p][1], back_pieces[p][3])
         return pltpu.make_async_remote_copy(
-            src_ref=back_v.at[d, :, at], dst_ref=returned_hbm.at[src, :, at],
+            src_ref=back_v.at[d, :, at], dst_ref=returned_v.at[src, :, at],
             send_sem=back_send_sem.at[p, d], recv_sem=back_recv_sem.at[p, src],
             device_id={"exp": d}, device_id_type=MESH,
-        )
-
-    def own_copy(p):
-        at = pl.ds(pieces[p][1], pieces[p][3])
-        return pltpu.make_async_copy(
-            back_v.at[me, :, at], returned_hbm.at[me, :, at], own_sem.at[p]
         )
 
     for p, piece in forward:
@@ -269,34 +262,37 @@
             rows = x_v[g * GROUP * CAP : (g + 1) * GROUP * CAP, low : low + segs * seg_w]
             back_v[g * GROUP : (g + 1) * GROUP, :, slab_lanes(piece)] = pack(rows, piece)
         others(lambda d, p=p: back_copy(p, d, me).start())
-        own_copy(p).start()
-
-    mixing_out.wait()
-    load_out.wait()
+        returned_v[me, :, slab_lanes(piece)] = back_v[me, :, slab_lanes(piece)]
+
+    for p, piece in forward:
+        others(lambda d, p=p: back_copy(p, d, d).wait_recv())
+        combine(piece, returned_v, mixing_v, out_ref)
     others(lambda d: mass_copy(d, d).wait_send())
+    for p, _ in backward:
+        others(lambda d, p=p: token_copy(p, d, d).wait_send())
     for p, _ in forward:
-        others(lambda d, p=p: token_copy(p, d, d).wait_send())
         others(lambda d, p=p: back_copy(p, d, d).wait_send())
-        own_copy(p).wait()
-    for p, _ in forward:
-        others(lambda d, p=p: back_copy(p, d, d).wait_recv())
-
-
-def combine(pieces, returned_ref, mixing_ref, load_in, out_ref, load_out):
+
+
+def combine(piece, returned_ref, mixing_ref, out_ref):
+    low, lane, segs, seg_w = piece
     tok_rows = out_ref.shape[0]
     groups, _, depth = mixing_ref.shape
-    for low, lane, segs, seg_w in pieces:
-        mixed = jnp.zeros((segs * tok_rows, seg_w), F32)
-        for g in range(groups):
-            slabs = returned_ref[g * GROUP : (g + 1) * GROUP, :, lane : lane + seg_w]
-            slabs = slabs.reshape(depth // 2, seg_w)
-            mixing = mixing_ref[g, : segs * tok_rows, :]
-            mixed = mixed + dot(mixing, jnp.concatenate([slabs, slabs], axis=0))
-        for s in range(segs):
-            out_ref[:, low + s * seg_w : low + (s + 1) * seg_w] = mixed[
-                s * tok_rows : (s + 1) * tok_rows
-            ].astype(BF16)
-    load_out[...] = load_in[...].reshape(EXPERTS_ALL)
+    mixed = jnp.zeros((segs * tok_rows, seg_w), F32)
+    for g in range(groups):
+        slabs = returned_ref[g * GROUP : (g + 1) * GROUP, :, lane : lane + seg_w]
+        slabs = slabs.reshape(depth // 2, seg_w)
+        mixing = mixing_ref[g, : segs * tok_rows, :]
+        mixed = mixed + dot(mixing, jnp.concatenate([slabs, slabs], axis=0))
+    for s in range(segs):
+        out_ref[:, low + s * seg_w : low + (s + 1) * seg_w] = mixed[
+            s * tok_rows : (s + 1) * tok_rows
+        ].astype(BF16)
+
+
+def copy_out(combined_in, load_in, combined_out, load_out):
+    combined_out[...] = combined_in[...]
+    load_out[...] = load_in[...]
 
 
 def shards(tokens, expert_ids, gate_scores, gate_weight, up_weight, down_weight):
@@ -304,11 +300,11 @@
     tok_rows, width = tokens.shape
     hid_dev = gate_weight.shape[1]
     spread = FF // hid_dev
-    pieces = cut(width)
-    count = len(pieces)
-    slab_w = pieces[-1][1] + pieces[-1][3]
+    pieces, back_pieces = cut(width, False), cut(width, True)
+    count, back_count = len(pieces), len(back_pieces)
+    slab_w = max(lane + seg_w for _, lane, _, seg_w in pieces + back_pieces)
     groups = n // GROUP
-    cfg = (n, spread, pieces)
+    cfg = (n, spread, pieces, back_pieces)
     dma = pltpu.SemaphoreType.DMA
     slabs = (n, SLAB, slab_w)
     mixing = (groups, SEGS * tok_rows, 2 * GROUP * SLAB)
@@ -322,8 +318,8 @@
         pltpu.VMEM(slabs, BF16),
         pltpu.VMEM(slabs, BF16),
         pltpu.VMEM(slabs, BF16),
+        pltpu.VMEM(slabs, BF16),
         pltpu.VMEM((n, 1, EXPERTS_ALL), F32),
-        pltpu.VMEM((1, EXPERTS_ALL), F32),
         pltpu.VMEM(mixing, BF16),
         pltpu.VMEM((n * CAP, width), BF16),
         pltpu.VMEM((n * CAP, hid_dev), F32),
@@ -332,41 +328,33 @@
         dma((3,)),
         dma((count, -(-width // BLOCK))),
         dma((count, -(-width // BLOCK))),
-        dma((count, -(-hid_dev // BLOCK))),
-        dma((2,)),
-        dma((count,)),
+        dma((back_count, -(-hid_dev // BLOCK))),
         dma((count, n)),
         dma((count, n)),
         dma((n,)),
         dma((n,)),
-        dma((count, n)),
-        dma((count, n)),
+        dma((back_count, n)),
+        dma((back_count, n)),
     ]
     vmem = pl.BlockSpec(memory_space=pltpu.VMEM)
     hbm = pl.BlockSpec(memory_space=pltpu.HBM)
-    partials = pl.pallas_call(
+    out_shape = (
+        jax.ShapeDtypeStruct(tokens.shape, BF16),
+        jax.ShapeDtypeStruct((EXPERTS_ALL,), F32),
+    )
+    results = pl.pallas_call(
         functools.partial(kernel, cfg),
-        out_shape=(
-            jax.ShapeDtypeStruct(slabs, BF16),
-            jax.ShapeDtypeStruct(mixing, BF16),
-            jax.ShapeDtypeStruct((1, EXPERTS_ALL), F32),
-        ),
+        out_shape=out_shape,
         in_specs=[hbm] * 6,
-        out_specs=(hbm, hbm, hbm),
+        out_specs=(vmem, vmem),
         scratch_shapes=scratch,
         compiler_params=pltpu.CompilerParams(
             collective_id=0, has_side_effects=True, vmem_limit_bytes=62 * 1024 * 1024
         ),
     )(tokens, expert_ids.T, gate_scores.T, gate_weight, up_weight, down_weight)
     return pl.pallas_call(
-        functools.partial(combine, pieces),
-        out_shape=(
-            jax.ShapeDtypeStruct(tokens.shape, BF16),
-            jax.ShapeDtypeStruct((EXPERTS_ALL,), F32),
-        ),
-        in_specs=[vmem] * 3,
-        out_specs=(vmem, vmem),
-    )(*partials)
+        copy_out, out_shape=out_shape, in_specs=[vmem, vmem], out_specs=(vmem, vmem)
+    )(*results)
 
 
 def solution(mesh):

time: 29.1 us -> 30.6 us (1.052)
  Pallas kernels: 28.3 us -> 29.8 us
    pallas_call x2, Pallas kernels: 28.3 us -> 29.8 us  [the longest x1 28.2 us: shards(): pl.pallas_call(functools.partial(kernel, cfg), out_shape=out_shape, in_sp...]
where the time goes in v7:
time: 30.6 us; the launch traced here: 30.4 us
  Pallas kernels  29.8 us (97%)
  between operations  0.64 us (2%)
    pallas_call x1, Pallas kernels, shards(): pl.pallas_call(functools.partial(kernel, cfg), out_shape=out_shape, in_sp...  28.2 us
    pallas_call x1, Pallas kernels, shards(): pl.pallas_call(copy_out, out_shape=out_shape, in_specs=[vmem, vmem], out_...  1.65 us

profile of v7, /device:TPU:0, one launch (start us, length us, event | category | flops | bytes accessed | tf_op | source)
XLA Modules:
  0.0 30.4 jit_solution(287865430610735673)
XLA Ops:
  0.6 28.2 %shard_map.77 = (bf16[32,3584]{1,0:T(8,128)(2,1)}, f32[384]{0:T(512)}) custom-call(bf16[32,3584]{1,0:T(8,128)(2,1)} %tokens_hbm.1, s32[8,32]{1,0:T(8,128)} %bitcast.2, f32[8,32]{1,0:T(8,128)} %bitcast.3, bf16[3584,2048]{1,0:T(8,128)(2,1)} %gate_hbm.1, bf16[3584,2048]{1,0:T(8,128)(2,1)} %up_hbm.1, bf16[2048,3584]{1,0:T(8,128)(2,1)} %down_hbm.1), custom_call_target="tpu_custom_call" | custom-call | tf_op jit(solution)/shard_map/pallas_call | solution.py:345
  28.8 1.6 %shard_map.78 = (bf16[32,3584]{1,0:T(8,128)(2,1)}, f32[384]{0:T(512)}) custom-call(bf16[32,3584]{1,0:T(8,128)(2,1)} %get-tuple-element.4.combined_in, f32[384]{0:T(512)} %get-tuple-element.5.load_in), custom_call_target="tpu_custom_call" | custom-call | tf_op jit(solution)/shard_map/pallas_call | solution.py:355

commit v8 on v3

--- a/solution.py
+++ b/solution.py
@@ -42,12 +42,11 @@
     tokens_v, ids_v, scores_v, gate_v, up_v, down_v,
     send_v, arrived_v, back_v, returned_v, mass_v, mixing_v, x_v, gate_sum, up_sum, hidden_v,
     small_sem, gate_sem, up_sem, down_sem,
-    send_sem, recv_sem, mass_send_sem, mass_recv_sem, back_send_sem, back_recv_sem,
+    send_sem, recv_sem, back_send_sem, back_recv_sem,
 ):
     n, spread, segs, pieces, piece_w, seg_w = cfg
     groups = n // GROUP
     top, tok_rows = ids_v.shape
-    lanes = mixing_lanes(n)
     me = lax.axis_index("exp")
 
     small = [
@@ -86,27 +85,16 @@
     barrier = pltpu.get_barrier_semaphore()
     others(lambda d: pl.semaphore_signal(barrier, inc=1, device_id={"exp": d}, device_id_type=MESH))
 
-    for copy in small[:2]:
-        copy.wait()
-    ids = jnp.transpose(ids_v[...])
-    scores = jnp.transpose(scores_v[...])
-    all_ids = iota((tok_rows, EXPERTS_ALL), 1)
-    slot = iota((tok_rows, lanes), 1)
-    slot_expert = jnp.where(slot < n * CAP, slot // (CAP * spread), -1)
-    mass = jnp.zeros((tok_rows, EXPERTS_ALL), F32)
-    gates = jnp.zeros((tok_rows, lanes), F32)
-    hits = jnp.zeros((tok_rows, lanes), F32)
+    small[0].wait()
+    slots = (n * CAP, tok_rows)
+    slot_expert = iota(slots, 0) // (CAP * spread)
+    hits = jnp.zeros(slots, F32)
     for k in range(top):
-        id_k, score_k = ids[:, k : k + 1], scores[:, k : k + 1]
-        mass = mass + jnp.where(id_k == all_ids, score_k, 0.0)
-        found = id_k == slot_expert
-        gates = gates + jnp.where(found, score_k, 0.0)
-        hits = hits + jnp.where(found, 1.0, 0.0)
-    earlier = one_hot(iota((tok_rows, tok_rows), 1) < iota((tok_rows, tok_rows), 0))
-    position = dot(earlier, hits.astype(BF16))
-    placed = (hits > 0.5) & (position == (slot % CAP).astype(F32))
-    picker = jnp.transpose(jnp.where(placed, 1.0, 0.0)).astype(BF16)
-    mass_v[me] = jnp.sum(mass, axis=0, keepdims=True)
+        hits = hits + jnp.where(ids_v[k : k + 1, :] == slot_expert, 1.0, 0.0)
+    earlier = one_hot(iota((tok_rows, tok_rows), 0) < iota((tok_rows, tok_rows), 1))
+    position = dot(hits.astype(BF16), earlier)
+    placed = (hits > 0.5) & (position == (iota(slots, 0) % CAP).astype(F32))
+    picker = one_hot(placed)
 
     slab_rows, packed_rows = GROUP * SLAB, segs * GROUP * CAP
     to_slab = one_hot(
@@ -118,7 +106,7 @@
 
     def pack(rows):
         packed = jnp.concatenate([rows[:, s * seg_w : (s + 1) * seg_w] for s in range(segs)], axis=0)
-        return dot(to_slab, packed).astype(BF16).reshape(GROUP, SLAB, seg_w)
+        return dot(to_slab, packed)
 
     small[2].wait()
     tokens = tokens_v[...]
@@ -126,44 +114,58 @@
         rows = picker[g * GROUP * CAP : (g + 1) * GROUP * CAP]
         picked = dot(rows, tokens).astype(BF16)
         for p in range(pieces):
-            slabs = pack(picked[:, p * piece_w : (p + 1) * piece_w])
-            send_v[p, g * GROUP : (g + 1) * GROUP] = slabs
-
-    def token_copy(p, d, src):
+            slabs = pack(picked[:, p * piece_w : (p + 1) * piece_w]).astype(BF16)
+            send_v[g * GROUP : (g + 1) * GROUP, :, p * seg_w : (p + 1) * seg_w] = slabs.reshape(
+                GROUP, SLAB, seg_w
+            )
+
+    def token_copy(d, src):
         return pltpu.make_async_remote_copy(
-            src_ref=send_v.at[p, d], dst_ref=arrived_v.at[p, src],
-            send_sem=send_sem.at[p, d], recv_sem=recv_sem.at[p, src],
+            src_ref=send_v.at[d], dst_ref=arrived_v.at[src],
+            send_sem=send_sem.at[d], recv_sem=recv_sem.at[src],
             device_id={"exp": d}, device_id_type=MESH,
         )
 
-    def mass_copy(d, src):
-        return pltpu.make_async_remote_copy(
-            src_ref=mass_v.at[me], dst_ref=mass_v.at[src],
-            send_sem=mass_send_sem.at[d], recv_sem=mass_recv_sem.at[src],
-            device_id={"exp": d}, device_id_type=MESH,
-        )
-
     pl.semaphore_wait(barrier, n - 1)
-    for p in range(pieces):
-        others(lambda d, p=p: token_copy(p, d, me).start())
-        arrived_v[p, me] = send_v[p, me]
+    others(lambda d: token_copy(d, me).start())
     for p in range(1, pieces):
         gate_copy(p).start()
         up_copy(p).start()
     for p in range(pieces):
         down_copy(p).start()
-    others(lambda d: mass_copy(d, me).start())
-
+    arrived_v[me] = send_v[me]
+
+    small[1].wait()
+    ids = jnp.transpose(ids_v[...])
+    scores = jnp.transpose(scores_v[...])
+    mass_w = pieces * seg_w
+    all_ids = iota((tok_rows, mass_w), 1)
+    mass = jnp.zeros((tok_rows, mass_w), F32)
+    for k in range(top):
+        mass = mass + jnp.where(ids[:, k : k + 1] == all_ids, scores[:, k : k + 1], 0.0)
+    mass = jnp.sum(mass, axis=0, keepdims=True)
+    mass_hi = mass.astype(BF16).astype(F32)
+    mass_v[0:1] = mass_hi
+    mass_v[1:2] = mass - mass_hi
+    slab_row = iota((slab_rows, seg_w), 0) % SLAB
+    hi_row, lo_row = slab_row == SLAB - 2, slab_row == SLAB - 1
+
+    gates = jnp.zeros(slots, F32)
+    for k in range(top):
+        found = ids_v[k : k + 1, :] == slot_expert
+        gates = gates + jnp.where(found, scores_v[k : k + 1, :], 0.0)
     weights = jnp.where(placed, gates, 0.0)
     weights_hi = weights.astype(BF16)
     weights_lo = (weights - weights_hi.astype(F32)).astype(BF16)
-    slab_lane = iota((lanes, slab_rows), 1)
+    slab_lane = iota((n * CAP, slab_rows), 1)
     lane_seg = (iota((tok_rows, slab_rows), 1) % SLAB) // CAP
     for g in range(groups):
         slot_of = g * GROUP * CAP + slab_lane // SLAB * CAP + slab_lane % CAP
-        spreading = one_hot(iota((lanes, slab_rows), 0) == slot_of)
+        spreading = one_hot(iota((n * CAP, slab_rows), 0) == slot_of)
         for part, term in enumerate((weights_hi, weights_lo)):
-            wide = dot(term, spreading)
+            wide = lax.dot_general(
+                term, spreading, (((0,), (0,)), ((), ())), preferred_element_type=F32
+            )
             for s in range(segs):
                 mixing_v[
                     g, s * tok_rows : (s + 1) * tok_rows, part * slab_rows : (part + 1) * slab_rows
@@ -171,11 +173,11 @@
 
     hid_dev = hidden_v.shape[1]
     hid_tile = min(TILE, hid_dev)
-    for p in range(pieces):
-        others(lambda d, p=p: token_copy(p, d, d).wait_recv())
+    others(lambda d: token_copy(d, d).wait_recv())
+    for p in range(pieces):
         for g in range(groups):
-            slabs = arrived_v[p, g * GROUP : (g + 1) * GROUP].reshape(slab_rows, seg_w)
-            packed = dot(from_slab, slabs).astype(BF16)
+            slabs = arrived_v[g * GROUP : (g + 1) * GROUP, :, p * seg_w : (p + 1) * seg_w]
+            packed = dot(from_slab, slabs.reshape(slab_rows, seg_w)).astype(BF16)
             size = GROUP * CAP
             for s in range(segs):
                 x_v[g * size : (g + 1) * size, s * seg_w : (s + 1) * seg_w] = packed[
@@ -215,31 +217,32 @@
             x_v[:, cols] = dot(hidden_v[...], down_v[p, :, cols]).astype(BF16)
         for g in range(groups):
             rows = x_v[g * GROUP * CAP : (g + 1) * GROUP * CAP]
-            back_v[p, g * GROUP : (g + 1) * GROUP] = pack(rows)
+            at = slice(p * seg_w, (p + 1) * seg_w)
+            spare = jnp.where(lo_row, mass_v[1:2, at], jnp.where(hi_row, mass_v[0:1, at], 0.0))
+            slabs = (pack(rows) + spare).astype(BF16)
+            back_v[p, g * GROUP : (g + 1) * GROUP] = slabs.reshape(GROUP, SLAB, seg_w)
         others(lambda d, p=p: back_copy(p, d, me).start())
         returned_v[p, me] = back_v[p, me]
 
-    others(lambda d: mass_copy(d, d).wait_recv())
-    load_ref[...] = jnp.sum(mass_v[...], axis=0).reshape(EXPERTS_ALL)
-
+    load = []
     for p in range(pieces):
         others(lambda d, p=p: back_copy(p, d, d).wait_recv())
         mixed = jnp.zeros((segs * tok_rows, seg_w), F32)
         for g in range(groups):
             slabs = returned_v[p, g * GROUP : (g + 1) * GROUP].reshape(slab_rows, seg_w)
             mixed = mixed + dot(mixing_v[g], jnp.concatenate([slabs, slabs], axis=0))
+            part = jnp.sum(jnp.where(hi_row | lo_row, slabs.astype(F32), 0.0), axis=0, keepdims=True)
+            total = part if g == 0 else total + part
+        load.append(total)
         for s in range(segs):
             low = p * piece_w + s * seg_w
             out_ref[:, low : low + seg_w] = mixed[s * tok_rows : (s + 1) * tok_rows].astype(BF16)
 
-    others(lambda d: mass_copy(d, d).wait_send())
-    for p in range(pieces):
-        others(lambda d, p=p: token_copy(p, d, d).wait_send())
+    load_ref[...] = jnp.concatenate(load, axis=1)[:, :EXPERTS_ALL].reshape(EXPERTS_ALL)
+
+    others(lambda d: token_copy(d, d).wait_send())
+    for p in range(pieces):
         others(lambda d, p=p: back_copy(p, d, d).wait_send())
-
-
-def mixing_lanes(n):
-    return -(-n * CAP // 128) * 128
 
 
 def copy_out(combined_in, load_in, combined_out, load_out):
@@ -267,11 +270,11 @@
         pltpu.VMEM((pieces, piece_w, hid_dev), BF16),
         pltpu.VMEM((pieces, piece_w, hid_dev), BF16),
         pltpu.VMEM((pieces, hid_dev, piece_w), BF16),
+        pltpu.VMEM((n, SLAB, pieces * seg_w), BF16),
+        pltpu.VMEM((n, SLAB, pieces * seg_w), BF16),
         pltpu.VMEM((pieces, n, SLAB, seg_w), BF16),
         pltpu.VMEM((pieces, n, SLAB, seg_w), BF16),
-        pltpu.VMEM((pieces, n, SLAB, seg_w), BF16),
-        pltpu.VMEM((pieces, n, SLAB, seg_w), BF16),
-        pltpu.VMEM((n, 1, EXPERTS_ALL), F32),
+        pltpu.VMEM((SLAB // 2, pieces * seg_w), F32),
         pltpu.VMEM((groups, segs * tok_rows, 2 * GROUP * SLAB), BF16),
         pltpu.VMEM((n * CAP, piece_w), BF16),
         pltpu.VMEM((n * CAP, hid_dev), F32),
@@ -281,8 +284,6 @@
         dma((pieces,)),
         dma((pieces,)),
         dma((pieces,)),
-        dma((pieces, n)),
-        dma((pieces, n)),
         dma((n,)),
         dma((n,)),
         dma((pieces, n)),

time: 28.5 us -> 28.2 us (0.989)
  Pallas kernels: 27.7 us -> 27.4 us
    pallas_call x1, Pallas kernels: 26.1 us -> 25.8 us  [shards(): pl.pallas_call(functools.partial(kernel, cfg), out_shape=out_shape, in_sp...]
where the time goes in v8:
time: 28.2 us; the launch traced here: 28 us
  Pallas kernels  27.4 us (97%)
  between operations  0.64 us (2%)
    pallas_call x1, Pallas kernels, shards(): pl.pallas_call(functools.partial(kernel, cfg), out_shape=out_shape, in_sp...  25.8 us
    pallas_call x1, Pallas kernels, shards(): pl.pallas_call(copy_out, out_shape=out_shape, in_specs=[vmem, vmem], out_...  1.65 us

profile of v8, /device:TPU:0, one launch (start us, length us, event | category | flops | bytes accessed | tf_op | source)
XLA Modules:
  0.0 28.0 jit_solution(16011515424853031374)
XLA Ops:
  0.6 25.8 %shard_map.77 = (bf16[32,3584]{1,0:T(8,128)(2,1)}, f32[384]{0:T(512)}) custom-call(bf16[32,3584]{1,0:T(8,128)(2,1)} %tokens_hbm.1, s32[8,32]{1,0:T(8,128)} %bitcast.2, f32[8,32]{1,0:T(8,128)} %bitcast.3, bf16[3584,2048]{1,0:T(8,128)(2,1)} %gate_hbm.1, bf16[3584,2048]{1,0:T(8,128)(2,1)} %up_hbm.1, bf16[2048,3584]{1,0:T(8,128)(2,1)} %down_hbm.1), custom_call_target="tpu_custom_call" | custom-call | tf_op jit(solution)/shard_map/pallas_call | solution.py:297
  26.4 1.6 %shard_map.78 = (bf16[32,3584]{1,0:T(8,128)(2,1)}, f32[384]{0:T(512)}) custom-call(bf16[32,3584]{1,0:T(8,128)(2,1)} %get-tuple-element.4.combined_in, f32[384]{0:T(512)} %get-tuple-element.5.load_in), custom_call_target="tpu_custom_call" | custom-call | tf_op jit(solution)/shard_map/pallas_call | solution.py:307

commit v9 on v8

--- a/solution.py
+++ b/solution.py
@@ -40,11 +40,12 @@
     tokens_hbm, ids_hbm, scores_hbm, gate_hbm, up_hbm, down_hbm,
     out_ref, load_ref,
     tokens_v, ids_v, scores_v, gate_v, up_v, down_v,
-    send_v, arrived_v, back_v, returned_v, mass_v, mixing_v, x_v, gate_sum, up_sum, hidden_v,
+    send_v, arrived_v, back_v, returned_v, mass_v, mixing_v, x_v, gate_sum, up_sum, hidden_v, down_sum,
     small_sem, gate_sem, up_sem, down_sem,
     send_sem, recv_sem, back_send_sem, back_recv_sem,
 ):
-    n, spread, segs, pieces, piece_w, seg_w = cfg
+    n, spread, segs, pieces, piece_w, seg_w, k_parts = cfg
+    k_rows = down_hbm.shape[0] // k_parts
     groups = n // GROUP
     top, tok_rows = ids_v.shape
     me = lax.axis_index("exp")
@@ -67,10 +68,9 @@
             up_hbm.at[pl.ds(p * piece_w, piece_w), :], up_v.at[p], up_sem.at[p]
         )
 
-    def down_copy(p):
-        return pltpu.make_async_copy(
-            down_hbm.at[:, pl.ds(p * piece_w, piece_w)], down_v.at[p], down_sem.at[p]
-        )
+    def down_copy(k):
+        rows = pl.ds(k * k_rows, k_rows)
+        return pltpu.make_async_copy(down_hbm.at[rows, :], down_v.at[rows, :], down_sem.at[k])
 
     gate_copy(0).start()
     up_copy(0).start()
@@ -131,8 +131,8 @@
     for p in range(1, pieces):
         gate_copy(p).start()
         up_copy(p).start()
-    for p in range(pieces):
-        down_copy(p).start()
+    for k in range(k_parts):
+        down_copy(k).start()
     arrived_v[me] = send_v[me]
 
     small[1].wait()
@@ -210,11 +210,24 @@
             device_id={"exp": d}, device_id_type=MESH,
         )
 
+    def down(k, cols):
+        at = slice(k * k_rows, (k + 1) * k_rows)
+        return dot(hidden_v[:, at], down_v[at, cols])
+
+    for k in range(k_parts - 1):
+        down_copy(k).wait()
+        for s in range(pieces * segs):
+            cols = slice(s * seg_w, (s + 1) * seg_w)
+            down_sum[:, cols] = down(k, cols) if k == 0 else down_sum[:, cols] + down(k, cols)
+    down_copy(k_parts - 1).wait()
     for p in range(pieces):
-        down_copy(p).wait()
         for s in range(segs):
-            cols = slice(s * seg_w, (s + 1) * seg_w)
-            x_v[:, cols] = dot(hidden_v[...], down_v[p, :, cols]).astype(BF16)
+            low = p * piece_w + s * seg_w
+            cols = slice(low, low + seg_w)
+            total = down(k_parts - 1, cols)
+            if k_parts > 1:
+                total = down_sum[:, cols] + total
+            x_v[:, s * seg_w : (s + 1) * seg_w] = total.astype(BF16)
         for g in range(groups):
             rows = x_v[g * GROUP * CAP : (g + 1) * GROUP * CAP]
             at = slice(p * seg_w, (p + 1) * seg_w)
@@ -261,7 +274,8 @@
     piece_w = width // pieces
     seg_w = piece_w // segs
     groups = n // GROUP
-    cfg = (n, spread, segs, pieces, piece_w, seg_w)
+    k_parts = 2 if hid_dev % 512 == 0 else 1
+    cfg = (n, spread, segs, pieces, piece_w, seg_w, k_parts)
     dma = pltpu.SemaphoreType.DMA
     scratch = [
         pltpu.VMEM(tokens.shape, BF16),
@@ -269,7 +283,7 @@
         pltpu.VMEM(gate_scores.shape[::-1], F32),
         pltpu.VMEM((pieces, piece_w, hid_dev), BF16),
         pltpu.VMEM((pieces, piece_w, hid_dev), BF16),
-        pltpu.VMEM((pieces, hid_dev, piece_w), BF16),
+        pltpu.VMEM((hid_dev, width), BF16),
         pltpu.VMEM((n, SLAB, pieces * seg_w), BF16),
         pltpu.VMEM((n, SLAB, pieces * seg_w), BF16),
         pltpu.VMEM((pieces, n, SLAB, seg_w), BF16),
@@ -280,10 +294,11 @@
         pltpu.VMEM((n * CAP, hid_dev), F32),
         pltpu.VMEM((n * CAP, hid_dev), F32),
         pltpu.VMEM((n * CAP, hid_dev), BF16),
+        pltpu.VMEM((n * CAP, width), F32),
         dma((3,)),
         dma((pieces,)),
         dma((pieces,)),
-        dma((pieces,)),
+        dma((k_parts,)),
         dma((n,)),
         dma((n,)),
         dma((pieces, n)),

time: 28.2 us -> 28.3 us (level)
  no operation moved by 1% of the time
where the time goes in v9:
time: 28.3 us; the launch traced here: 28.1 us
  Pallas kernels  27.5 us (97%)
  between operations  0.64 us (2%)
    pallas_call x1, Pallas kernels, shards(): pl.pallas_call(functools.partial(kernel, cfg), out_shape=out_shape, in_sp...  25.8 us
    pallas_call x1, Pallas kernels, shards(): pl.pallas_call(copy_out, out_shape=out_shape, in_specs=[vmem, vmem], out_...  1.65 us

profile of v9, /device:TPU:0, one launch (start us, length us, event | category | flops | bytes accessed | tf_op | source)
XLA Modules:
  0.0 28.1 jit_solution(8802786133718148412)
XLA Ops:
  0.6 25.8 %shard_map.77 = (bf16[32,3584]{1,0:T(8,128)(2,1)}, f32[384]{0:T(512)}) custom-call(bf16[32,3584]{1,0:T(8,128)(2,1)} %tokens_hbm.1, s32[8,32]{1,0:T(8,128)} %bitcast.2, f32[8,32]{1,0:T(8,128)} %bitcast.3, bf16[3584,2048]{1,0:T(8,128)(2,1)} %gate_hbm.1, bf16[3584,2048]{1,0:T(8,128)(2,1)} %up_hbm.1, bf16[2048,3584]{1,0:T(8,128)(2,1)} %down_hbm.1), custom_call_target="tpu_custom_call" | custom-call | tf_op jit(solution)/shard_map/pallas_call | solution.py:312
  26.5 1.6 %shard_map.78 = (bf16[32,3584]{1,0:T(8,128)(2,1)}, f32[384]{0:T(512)}) custom-call(bf16[32,3584]{1,0:T(8,128)(2,1)} %get-tuple-element.4.combined_in, f32[384]{0:T(512)} %get-tuple-element.5.load_in), custom_call_target="tpu_custom_call" | custom-call | tf_op jit(solution)/shard_map/pallas_call | solution.py:322

commit v10 on v8

--- a/solution.py
+++ b/solution.py
@@ -12,7 +12,7 @@
 CAP = 2
 SLAB = 16
 GROUP = 8
-TILE = 256
+TILE = 512
 MESH = pl.DeviceIdType.MESH
 BF16 = jnp.bfloat16
 F32 = jnp.float32
@@ -201,7 +201,7 @@
                 hidden_v[:, cols] = (silu * up_act).astype(BF16)
             return carry
 
-        lax.fori_loop(0, hid_dev // hid_tile, gate_up, 0)
+        lax.fori_loop(0, hid_dev // hid_tile, gate_up, 0, unroll=2 if hid_dev > hid_tile else 1)
 
     def back_copy(p, d, src):
         return pltpu.make_async_remote_copy(

time: 28.2 us -> 27.3 us (0.968)
  Pallas kernels: 27.4 us -> 26.5 us
    pallas_call x1, Pallas kernels: 25.8 us -> 24.8 us  [shards(): pl.pallas_call(functools.partial(kernel, cfg), out_shape=out_shape, in_sp...]
where the time goes in v10:
time: 27.3 us; the launch traced here: 27.1 us
  Pallas kernels  26.5 us (97%)
  between operations  0.64 us (2%)
    pallas_call x1, Pallas kernels, shards(): pl.pallas_call(functools.partial(kernel, cfg), out_shape=out_shape, in_sp...  24.8 us
    pallas_call x1, Pallas kernels, shards(): pl.pallas_call(copy_out, out_shape=out_shape, in_specs=[vmem, vmem], out_...  1.65 us

profile of v10, /device:TPU:0, one launch (start us, length us, event | category | flops | bytes accessed | tf_op | source)
XLA Modules:
  0.0 27.1 jit_solution(14560897761349010429)
XLA Ops:
  0.6 24.8 %shard_map.77 = (bf16[32,3584]{1,0:T(8,128)(2,1)}, f32[384]{0:T(512)}) custom-call(bf16[32,3584]{1,0:T(8,128)(2,1)} %tokens_hbm.1, s32[8,32]{1,0:T(8,128)} %bitcast.2, f32[8,32]{1,0:T(8,128)} %bitcast.3, bf16[3584,2048]{1,0:T(8,128)(2,1)} %gate_hbm.1, bf16[3584,2048]{1,0:T(8,128)(2,1)} %up_hbm.1, bf16[2048,3584]{1,0:T(8,128)(2,1)} %down_hbm.1), custom_call_target="tpu_custom_call" | custom-call | tf_op jit(solution)/shard_map/pallas_call | solution.py:297
  25.5 1.6 %shard_map.78 = (bf16[32,3584]{1,0:T(8,128)(2,1)}, f32[384]{0:T(512)}) custom-call(bf16[32,3584]{1,0:T(8,128)(2,1)} %get-tuple-element.4.combined_in, f32[384]{0:T(512)} %get-tuple-element.5.load_in), custom_call_target="tpu_custom_call" | custom-call | tf_op jit(solution)/shard_map/pallas_call | solution.py:307
